TPU v7x, 256 devices: a whole 4x4x8 slice. The times are simulated.
256 devices in a mesh: branch: 16 (over z, core), tile: 16 (over x, y).
Axes of the slice: x: 4, y: 4, z: 8, core: 2. Of those that a mesh axis runs over, the one named last changes fastest.
Arguments:
- features: bfloat16 [16, 16, 1, 4096, 128], P('branch', 'tile'), may hold values from -6 to 6
- merge_local: bfloat16 [256, 128], replicated, may hold values from -0.375 to 0.375
- conv_local: bfloat16 [3, 3, 128, 128], replicated, may hold values from -0.1875 to 0.1875
- merge_global: bfloat16 [256, 128], replicated, may hold values from -0.375 to 0.375
- conv_global: bfloat16 [3, 3, 128, 128], replicated, may hold values from -0.1875 to 0.1875
- crop_offsets: int32 [15, 16, 1, 2], replicated, may hold values from 0 to 248, as said below
- crop_sizes: int32 [15, 16, 1, 2], replicated, may hold values from 8 to 16
- owners: int32 [15, 16, 1], replicated, may hold values from 0 to 15
Outputs:
- refined: bfloat16 [16, 16, 1, 4096, 128], P('branch', 'tile')
Inputs may be any that keep to these rules, and one draw needn't show every extreme that they name: `crop_offsets`: y0 + h <= 16 and x0 + w <= 256, with (h, w) the same tile's crop_sizes.
All inputs are finite; a program needn't handle non-finite values.
Results may differ from a plain program's by a relative error of at most 0.005.
Values may be sent and summed in bfloat16 or wider, within the bound.
A program may use at most 64 MiB of HBM per device.

v0:
```python
import jax
import jax.numpy as jnp
from jax import lax
from jax.sharding import PartitionSpec as P

S = 64
BAND_H = 16
GW = 256
WIN = 16


def spread(x, axis, root):
    mine = lax.axis_index(axis) == root
    return lax.psum(jnp.where(mine, x, jnp.zeros_like(x)), axis)


def with_halo(x, sides, width):
    for axis, dim in sides:
        size, length = (lax.axis_size(axis), x.shape[dim])
        up = [(i, (i + 1) % size) for i in range(size - 1)]
        down = [(j, i) for i, j in up]
        last = lax.slice_in_dim(x, length - width, length, axis=dim)
        initial = lax.slice_in_dim(x, 0, width, axis=dim)
        before = lax.ppermute(last, axis, up)
        after = lax.ppermute(initial, axis, down)
        x = jnp.concatenate([before, x, after], axis=dim)
    return x


def nearest_map(size_now, extent):
    targets = jnp.arange(WIN, dtype=jnp.int32)[:, None]
    sources = jnp.arange(extent, dtype=jnp.int32)[None, :]
    return (sources * size_now // extent == targets).astype(jnp.float32)


def pool_window(cells, row_size, col_size):
    row_map = nearest_map(row_size, S)
    col_map = nearest_map(col_size, S)
    colsum = jnp.einsum(
        "vj,ijc->ivc", col_map.astype(jnp.bfloat16), cells, preferred_element_type=jnp.float32
    )
    rowsum = jnp.einsum("ui,ivc->uvc", row_map, colsum, precision=lax.Precision.HIGHEST)
    counts = jnp.sum(row_map, axis=1)[:, None] * jnp.sum(col_map, axis=1)[None, :]
    return (rowsum / jnp.maximum(counts, 1.0)[:, :, None]).astype(jnp.bfloat16)


def crop_window(padded_band, top, left, row_size, col_size):
    root = jnp.zeros((), jnp.int32)
    sliced = lax.dynamic_slice(padded_band, (top, left, root), (WIN, WIN, padded_band.shape[2]))
    reach = jnp.arange(WIN, dtype=jnp.int32)
    inside = (reach < row_size)[:, None] & (reach < col_size)[None, :]
    return jnp.where(inside[:, :, None], sliced, jnp.zeros_like(sliced))


def upsample(crop_cells, row_size, col_size):
    row_map = nearest_map(row_size, S).astype(jnp.bfloat16)
    col_map = nearest_map(col_size, S).astype(jnp.bfloat16)
    rows_done = jnp.einsum(
        "ui,uvc->ivc", row_map, crop_cells, preferred_element_type=jnp.float32
    ).astype(jnp.bfloat16)
    return jnp.einsum("vj,ivc->ijc", col_map, rows_done, preferred_element_type=jnp.float32).astype(
        jnp.bfloat16
    )


def place_one(canvas, window, top, left):
    root = jnp.zeros((), jnp.int32)
    current = lax.dynamic_slice(canvas, (top, left, root), (WIN, WIN, canvas.shape[2]))
    return lax.dynamic_update_slice(canvas, current + window.astype(jnp.float32), (top, left, root))


def convolve(padded, kernel):
    span_rows = padded.shape[1] - 2
    span_cols = padded.shape[2] - 2
    summed = jnp.zeros((padded.shape[0] * span_rows * span_cols, kernel.shape[3]), jnp.float32)
    for row_step in range(3):
        for col_step in range(3):
            sliced = padded[
                :, row_step : row_step + span_rows, col_step : col_step + span_cols
            ].reshape(-1, padded.shape[3])
            summed = summed + jnp.dot(
                sliced, kernel[row_step, col_step], preferred_element_type=jnp.float32
            )
    return summed


def shards(
    features, merge_local, conv_local, merge_global, conv_global, crop_offsets, crop_sizes, owners
):
    planes = features[0, 0]
    images = planes.shape[0]
    channels = planes.shape[2]
    branch_count = lax.axis_size("branch")
    tile_count = lax.axis_size("tile")
    branch_id = lax.axis_index("branch")
    tile_id = lax.axis_index("tile")
    is_global = branch_id == branch_count - 1
    active = jnp.logical_not(is_global)
    slot_index = jnp.minimum(branch_id, branch_count - 2)
    slot_offsets = crop_offsets[slot_index]
    slot_sizes = crop_sizes[slot_index]
    slot_owners = owners[slot_index]
    own_sizes = slot_sizes[tile_id]
    own_owners = slot_owners[tile_id]
    tile_cells = planes.reshape(images, S, S, channels)
    windows = jax.vmap(pool_window)(tile_cells, own_sizes[:, 0], own_sizes[:, 1])
    target = (jnp.arange(tile_count, dtype=jnp.int32)[None, :] == own_owners[:, None]) & active
    outgoing = jnp.where(
        target[:, :, None, None, None], windows[:, None], jnp.zeros((), jnp.bfloat16)
    )
    arrived = lax.all_to_all(outgoing, "tile", split_axis=1, concat_axis=1, tiled=True)

    def visit(source, canvas):
        return jax.vmap(place_one)(
            canvas, arrived[:, source], slot_offsets[source, :, 0], slot_offsets[source, :, 1]
        )

    canvas_start = jnp.zeros((images, BAND_H + WIN, GW + WIN, channels), jnp.float32)
    partial_band = lax.fori_loop(0, tile_count, visit, canvas_start)[:, :BAND_H, :GW]
    band_cells = spread(planes, "branch", branch_count - 1)
    band_grid = band_cells.reshape(images, BAND_H, GW, channels)
    padded_band = jnp.pad(band_grid, ((0, 0), (0, WIN), (0, WIN), (0, 0)))
    requested = jax.vmap(
        jax.vmap(crop_window, in_axes=(None, 0, 0, 0, 0)), in_axes=(0, 1, 1, 1, 1)
    )(
        padded_band,
        slot_offsets[:, :, 0],
        slot_offsets[:, :, 1],
        slot_sizes[:, :, 0],
        slot_sizes[:, :, 1],
    )
    serve = ((slot_owners == tile_id) & active).T
    requested = jnp.where(serve[:, :, None, None, None], requested, jnp.zeros((), jnp.bfloat16))
    delivered = lax.all_to_all(requested, "tile", split_axis=1, concat_axis=1, tiled=True)
    crop_cells = jnp.sum(delivered.astype(jnp.float32), axis=1).astype(jnp.bfloat16)
    upsampled = jax.vmap(upsample)(crop_cells, own_sizes[:, 0], own_sizes[:, 1])
    local_joined = jnp.concatenate([tile_cells, upsampled], axis=-1).reshape(-1, 2 * channels)
    summed = lax.psum(partial_band.astype(jnp.bfloat16), "branch")
    global_joined = jnp.concatenate([band_grid, summed], axis=-1).reshape(-1, 2 * channels)
    joined = jnp.where(is_global, global_joined, local_joined)
    weight = jnp.where(is_global, merge_global, merge_local)
    merging = jax.nn.relu(jnp.dot(joined, weight, preferred_element_type=jnp.float32)).astype(
        jnp.bfloat16
    )
    merged_band = merging.reshape(images, BAND_H, GW, channels)
    rimmed = with_halo(merged_band, (("tile", 1),), 1)

    def global_conv(operands):
        rim_rows = operands[1]
        padded = jnp.pad(rim_rows, ((0, 0), (0, 0), (1, 1), (0, 0)))
        return convolve(padded, conv_global)

    def local_conv(operands):
        padded = jnp.pad(
            operands[0].reshape(images, S, S, channels), ((0, 0), (1, 1), (1, 1), (0, 0))
        )
        return convolve(padded, conv_local)

    result = lax.cond(is_global, global_conv, local_conv, (merging, rimmed))
    return result.astype(jnp.bfloat16).reshape(1, 1, images, S * S, channels)


def solution(mesh):
    in_specs = (P("branch", "tile", None, None, None), P(), P(), P(), P(), P(), P(), P())
    out_specs = P("branch", "tile", None, None, None)
    return jax.shard_map(shards, mesh=mesh, in_specs=in_specs, out_specs=out_specs, check_vma=False)
```

profile of v0, /device:TPU:1, one launch (start us, length us, event | category | flops | bytes accessed | tf_op | source)
XLA Modules:
  0.0 434.0 jit_solution(17290420743652929063)
XLA Ops:
  14.0 7.6 %all-to-all-start = ((bf16[1,16,16,16,128]{4,3,2,0,1:T(8,128)(2,1)}), bf16[1,16,16,16,128]{4,3,2,0,1:T(8,128)(2,1)S(1)}, u32[]{:S(2)}, u32[]{:S(2)}) async-start(bf16[1,16,16,16,128]{4,3,2,0,1:T(8,128)(2,1)} %copy.37), calls=%async_computation | async-start | bytes 2097152 | tf_op jit(solution)/shard_map/all_to_all | solution.py:111
  23.5 13.6 %all-to-all-done = bf16[1,16,16,16,128]{4,3,2,0,1:T(8,128)(2,1)S(1)} async-done(((bf16[1,16,16,16,128]{4,3,2,0,1:T(8,128)(2,1)}), bf16[1,16,16,16,128]{4,3,2,0,1:T(8,128)(2,1)S(1)}, u32[]{:S(2)}, u32[]{:S(2)}) %all-to-all-start) | async-done | bytes 1048608 | tf_op jit(solution)/shard_map/all_to_all | solution.py:111
  39.5 213.6 %while.15 = (s32[]{:T(128)}, f32[1,32,272,128]{3,2,1,0:T(8,128)}, s32[16,1,2]{0,2,1:T(2,128)S(1)}, bf16[1,16,16,16,128]{4,3,2,1,0:T(8,128)(2,1)S(1)}, s32[]{:T(1...) while((s32[]{:T(128)}, f32[1,32,272,128]{3,2,1,0:T(8,128)}, ...), condition=%wide.region_5.6_spmd, body=%wide.region_3.5_spmd.sunk | while | flops 98348 | bytes 721227 | solution.py:119
  47.0 2.9 fusion.97
  60.4 2.9 fusion.97
  73.7 2.9 fusion.97
  87.0 2.9 fusion.97
  100.4 2.9 fusion.97
  113.7 2.9 fusion.97
  127.1 2.9 fusion.97
  140.4 2.9 fusion.97
  167.1 2.9 fusion.97
  193.9 2.9 fusion.97
  207.2 2.9 fusion.97
  220.5 2.9 fusion.97
  247.3 2.9 fusion.97
  256.6 116.3 %all-reduce.6.cloned.1.call-done = (bf16[4096,128]{1,0:T(8,128)(2,1)}, bf16[1,4096,128]{2,1,0:T(8,128)(2,1)}) async-done(((bf16[4096,128]{1,0:T(8,128)(2,1)}, bf16[1,4096,128]{2,1,0:T(8,128)(2,1)}), (bf16[4096,128]{1,0:T(8,128)(2,1)}, bf16[1,4096,128]{2,1,0:T(8,128)(2,1)})) %all-reduce.6.cloned.1.call-update) | async-done | bytes 2097168 | tf_op jit(solution)/shard_map/psum | solution.py:138
  372.9 3.2 copy.39
  376.2 5.4 %pad.20 = bf16[1,32,272,128]{3,0,2,1:T(2,128)(2,1)} pad(bf16[1,16,256,128]{3,0,2,1:T(2,128)(2,1)S(1)} %copy.39, bf16[]{:T(256)} %constant.190.clone.1), padding=0_0x0_16x0_16x0_0 | pad | bytes 3276802 | tf_op jit(solution)/shard_map/jit(_pad)/pad | solution.py:122
  381.6 3.8 gather_fusion
  386.4 21.1 %all_to_all.10 = bf16[1,16,16,16,128]{4,3,2,0,1:T(8,128)(2,1)S(1)} all-to-all(bf16[1,16,16,16,128]{4,3,2,0,1:T(8,128)(2,1)S(1)} %copy.40), channel_id=1, replica_groups=mesh['branch'=16,'tile'=16] {'tile'}, dimensions={1} | all-to-all | bytes 2097152 | tf_op jit(solution)/shard_map/all_to_all | solution.py:134
  414.2 3.7 collective-permute-done.1
  418.0 7.4 %conditional.1 = (bf16[1,1,1,4096,128]{4,3,2,1,0:T(8,128)(2,1)S(1)}) conditional(s32[]{:T(128)} %convert_element_type.111, (bf16[4096,128]{1,0:T(8,128)(2,1)S(1)}, bf16[3,3,128,128]{3,2,1,0:T(8,128)(2,1)S(1)}) %tuple.96, (bf16[1,18,256,128]{3,2,1,0:T(8,128)(2,1)S(1)}, bf16[3,3,128,128]{3,2,1,0:T(8,128)(2,1)S(1)}) %tuple.97), branch_computations={%region_8.9_spmd, %region_9.10_spmd} | conditional | flops 1212678144 | bytes 58097672 | solution.py:159
  418.1 3.6 pad_slice_fusion
  (154 shorter events, 145.6 us)
Async XLA Ops:
  6.5 1.3 copy-start
  12.8 9.6 %copy-start.2 = (bf16[1,1,1,4096,128]{4,3,2,1,0:T(8,128)(2,1)S(1)}, bf16[1,1,1,4096,128]{4,3,2,1,0:T(8,128)(2,1)}, u32[]{:S(2)}) copy-start(bf16[1,1,1,4096,128]{4,3,2,1,0:T(8,128)(2,1)} %param.14) | copy-start | bytes 3145732
  14.0 23.1 %all-to-all-start = ((bf16[1,16,16,16,128]{4,3,2,0,1:T(8,128)(2,1)}), bf16[1,16,16,16,128]{4,3,2,0,1:T(8,128)(2,1)S(1)}, u32[]{:S(2)}, u32[]{:S(2)}) async-start(bf16[1,16,16,16,128]{4,3,2,0,1:T(8,128)(2,1)} %copy.37), calls=%async_computation | async-start | bytes 2097152 | tf_op jit(solution)/shard_map/all_to_all | solution.py:111
  21.6 351.3 %all-reduce.6.cloned.1.call-start = ((), (), s32[]{:S(2)}) async-start(), calls=%async_computation.2 | async-start | bytes 4194304 | tf_op jit(solution)/shard_map/psum | solution.py:138
  37.1 2.3 copy-start.7
  37.1 2.3 copy-start.8
  386.4 22.0 %copy-start.3 = (bf16[1,4096,128]{2,1,0:T(8,128)(2,1)S(1)}, bf16[1,4096,128]{2,1,0:T(8,128)(2,1)}, u32[]{:S(2)}) copy-start(bf16[1,4096,128]{2,1,0:T(8,128)(2,1)} %get-tuple-element.168) | copy-start | bytes 3145732
  386.4 22.0 %copy-start.9 = (bf16[256,128]{1,0:T(8,128)(2,1)S(1)}, bf16[256,128]{1,0:T(8,128)(2,1)}, u32[]{:S(2)}) copy-start(bf16[256,128]{1,0:T(8,128)(2,1)} %param.17) | copy-start | bytes 196612
  386.4 22.0 %copy-start.10 = (bf16[256,128]{1,0:T(8,128)(2,1)S(1)}, bf16[256,128]{1,0:T(8,128)(2,1)}, u32[]{:S(2)}) copy-start(bf16[256,128]{1,0:T(8,128)(2,1)} %param.15) | copy-start | bytes 196612
  410.5 7.5 %copy-start.5 = (bf16[3,3,128,128]{3,2,1,0:T(8,128)(2,1)S(1)}, bf16[3,3,128,128]{3,2,1,0:T(8,128)(2,1)}, u32[]{:S(2)}) copy-start(bf16[3,3,128,128]{3,2,1,0:T(8,128)(2,1)} %param.16) | copy-start | bytes 884740
  410.5 7.5 %copy-start.6 = (bf16[3,3,128,128]{3,2,1,0:T(8,128)(2,1)S(1)}, bf16[3,3,128,128]{3,2,1,0:T(8,128)(2,1)}, u32[]{:S(2)}) copy-start(bf16[3,3,128,128]{3,2,1,0:T(8,128)(2,1)} %param.18) | copy-start | bytes 884740
  410.5 3.6 collective-permute-start
  412.9 5.0 %collective-permute-start.1 = (bf16[1,1,256,128]{3,2,1,0:T(8,128)(2,1)S(1)}, bf16[1,1,256,128]{3,2,1,0:T(8,128)(2,1)S(1)}, u32[]{:S(2)}, u32[]{:S(2)}) collective-permute-start(bf16[1,1,256,128]{3,2,1,0:T(8,128)(2,1)S(1)} %get-tuple-element.192), channel_id=1, source_target_pairs={{1,0},{2,1},{3,2},{4,3},{5,4},{6,5},{7,6},{8,7},{9,8},{10,9},{11,1... | collective-permute-start | bytes 196616 | tf_op jit(solution)/shard_map/ppermute | solution.py:25
  425.4 1.0 copy-start.4
  426.4 0.7 copy-start.1
Sparse Core Ops, SparseCore 0:
  256.0 116.8 all-reduce.5
where the time goes:
time: 441 us; the launch traced here: 434 us
  waiting for transfers between devices  134 us (30%)
  other arithmetic  95 us (22%)
  local copies, waits for them, and re-layouts  92.8 us (21%)
  loops' own time  58.1 us (13%)
  blocking collectives  21.1 us (5%)
  between operations  13.7 us (3%)
  starting transfers between devices  11.2 us (3%)
  matrix products  8.36 us (2%)
    psum x1, waiting for transfers between devices, shards(): summed = lax.psum(partial_band.astype(jnp.bfloat16), 'branch')  116 us
    another operation x32, other arithmetic  88.6 us
    another operation x1, loops' own time, shards(): lax.fori_loop(0, tile_count, visit, canvas_start)[:, :BAND_H, :GW]  58.1 us
    scatter x16, local copies, waits for them, and re-layouts, place_one(): lax.dynamic_update_slice(canvas, current + window.astype(jnp.float32), (t...  46 us
    all_to_all x1, blocking collectives, shards(): lax.all_to_all(requested, 'tile', split_axis=1, concat_axis=1, tiled=True)  21.1 us
    all_to_all x1, waiting for transfers between devices, shards(): lax.all_to_all(outgoing, 'tile', split_axis=1, concat_axis=1, tiled=True)  13.6 us
    another operation x17, local copies, waits for them, and re-layouts  10.3 us
    dynamic_slice x16, local copies, waits for them, and re-layouts, visit(): slot_offsets[source, :, 1]  9.4 us
  transfers between devices with their start and end apart: 4, of which 3 were waited for; matrix products, arithmetic and copies ran while one was open for 1% of the time, Pallas kernels for 0%

commit v1 on v0

v1 whole, which is shorter than its diff:
```python
import functools

import jax
import jax.numpy as jnp
from jax import lax
from jax.experimental import pallas as pl
from jax.experimental.pallas import tpu as pltpu
from jax.sharding import PartitionSpec as P

MESH = pl.DeviceIdType.MESH
BF = jnp.bfloat16
F32 = jnp.float32
C = 128
S = 64
GW = 256
CELLS = 4096
HALF = 8
GROUPS = 2
GROUP = HALF // GROUPS
HOP = 3
GATHER1 = 5
GATHER2 = 12
REDUCE = 8


def band_row(q):
    return jnp.where(q < HALF, q, 3 * HALF - 1 - q)


def iota(shape, dim):
    return lax.broadcasted_iota(jnp.int32, shape, dim)


def kernel(
    n, nz, x_ref, ml_ref, cl_ref, mg_ref, cg_ref, off_ref, size_ref, own_ref, out_ref,
    win, wall, band, smat, pmat, canv, canv_in, rs1, rs1_in, rs2, rs2_in, root_b, halo, halo_out,
    crop, cu, zbuf, wlo, whi,
    bc_s, bc_s2, bc_r, a1_s, a1_r, a2_s, a2_r, cv_s, cv_r, rb_r, r1_s, r1_r, r2_s, r2_r, h_s, h_r,
):
    tiles = n * n
    ops = 2 * tiles
    br = lax.axis_index("branch")
    t = lax.axis_index("tile")
    z, c = br // 2, br % 2
    xx, yy = t // n, t % n
    up = c == 1
    f0 = jnp.where(up, xx, yy)
    g0 = jnp.where(up, yy, xx)
    pos = jnp.where(up, (z + 1) % nz, nz - 1 - z)
    z_next = jnp.where(up, (z + 1) % nz, (z + nz - 1) % nz)
    z_prev = jnp.where(up, (z + nz - 1) % nz, (z + 1) % nz)
    nxt = (2 * z_next + c, t)
    prv = (2 * z_prev + c, t)
    last = 2 * nz - 1
    is_root = br == last
    is_entry = br == last - 1
    half = 1 - c

    def tile_of(f, g):
        return jnp.where(up, f * n + g, g * n + f)

    def rc(src, dst, ss, rs, dev):
        return pltpu.make_async_remote_copy(
            src_ref=src, dst_ref=dst, send_sem=ss, recv_sem=rs, device_id=dev, device_id_type=MESH
        )

    barrier = pltpu.get_barrier_semaphore()

    def greet(dev):
        pl.semaphore_signal(barrier, inc=1, device_id=dev, device_id_type=MESH)

    greet(nxt)
    greet(prv)
    greet((2 * z + 1 - c, t))
    count = 3
    for core in (0, 1):
        for d in range(1, n):
            greet((2 * z + core, ((xx + d) % n) * n + yy))
            greet((2 * z + core, xx * n + (yy + d) % n))
            count += 2
    above = jnp.logical_and(is_root, t > 0)
    below = jnp.logical_and(is_root, t < tiles - 1)

    @pl.when(above)
    def _():
        greet((last, jnp.maximum(t - 1, 0)))

    @pl.when(below)
    def _():
        greet((last, jnp.minimum(t + 1, tiles - 1)))

    extra = jnp.where(above, 1, 0) + jnp.where(below, 1, 0)
    pl.semaphore_wait(barrier, count + extra)

    def x_row(r):
        return x_ref.at[pl.ds(pl.multiple_of(r * GW, GW), GW)]

    def root_up(k):
        return rc(x_row(k), band.at[k], bc_s.at[k], bc_r.at[k], nxt)

    def root_side(k):
        return rc(x_row(2 * HALF - 1 - k), band.at[k], bc_s2.at[k], bc_r.at[k], (last - 1, t))

    @pl.when(is_root)
    def _():
        for k in range(HALF):
            root_up(k).start()
            root_side(k).start()
        band[...] = x_ref[0 : HALF * GW].reshape(HALF, GW, C)

    slot = jnp.minimum(br, last - 1)
    top = off_ref[slot, t, 0, 0]
    hh = size_ref[slot, t, 0, 0]
    ww = size_ref[slot, t, 0, 1]

    sub = iota((256, 1), 0)
    sub_row = band_row(sub // 16) - top
    sub_col = sub % 16
    lane64 = iota((1, 128), 1)
    inside = lane64 < S
    row_hits = jnp.where(jnp.logical_and(inside, ((lane64 * hh) >> 6) == sub_row), 1.0, 0.0)
    col_hits = jnp.where(jnp.logical_and(inside, ((lane64 * ww) >> 6) == sub_col), 1.0, 0.0)
    counts = jnp.sum(row_hits, axis=1, keepdims=True) * jnp.sum(col_hits, axis=1, keepdims=True)
    wide = 1024
    lane = iota((1, wide), 1)
    cols = jnp.where((((lane % S) * ww) >> 6) == sub_col, 1.0, 0.0)

    def pool_step(step, acc):
        rows_at = ((step * (wide // S) + lane // S) * hh) >> 6
        lhs = jnp.where(rows_at == sub_row, cols, 0.0).astype(BF)
        rhs = x_ref[pl.ds(pl.multiple_of(step * wide, wide), wide)]
        return acc + jnp.dot(lhs, rhs, preferred_element_type=F32)

    pooled_win = lax.fori_loop(0, CELLS // wide, pool_step, jnp.zeros((256, C), F32))
    win[...] = (pooled_win / jnp.maximum(counts, 1.0)).astype(BF).reshape(16, 16, C)

    def gather1(d, core):
        if core == 1:
            peer = ((xx + d) % n) * n + yy
            dst = wall.at[yy, xx, c]
            src = win.at[0:HALF]
            sem = a1_r.at[xx, c]
        else:
            peer = xx * n + (yy + d) % n
            dst = wall.at[xx, yy, c]
            src = win.at[HALF : 2 * HALF]
            sem = a1_r.at[yy, c]
        return rc(src, dst, a1_s.at[core, d], sem, (2 * z + core, peer))

    for d in range(n):
        for core in (0, 1):
            if d:
                gather1(d, core).start()
            else:

                @pl.when(c != core)
                def _(d=d, core=core):
                    gather1(d, core).start()

    @pl.when(up)
    def _():
        wall[yy, xx, 1] = win[0:HALF]

    @pl.when(jnp.logical_not(up))
    def _():
        wall[xx, yy, 0] = win[HALF : 2 * HALF]

    diag = iota((16, GW), 1) - iota((16, GW), 0)
    lanes_op = iota((1, ops * 16), 1) // 16

    def select_step(i, at):
        f, rest = i // (2 * n), i % (2 * n)
        g, s = rest // 2, rest % 2
        tile = tile_of(f, g)
        b = 2 * z + s
        bb = jnp.minimum(b, last - 1)
        mine = jnp.logical_and(own_ref[bb, tile, 0] == t, b < last)
        left = jnp.where(mine, off_ref[bb, tile, 0, 1], -1024)
        smat[pl.ds(pl.multiple_of(i * 16, 16), 16)] = jnp.where(diag == left, 1.0, 0.0).astype(BF)
        return jnp.where(lanes_op == (g * n + f) * 2 + s, left, at)

    lefts = lax.fori_loop(0, ops, select_step, jnp.zeros((1, ops * 16), jnp.int32))
    lefts = lefts + iota((1, ops * 16), 1) % 16
    pmat[...] = jnp.where(iota((GW, 1), 0) == lefts, 1.0, 0.0).astype(BF)

    def conv_weights(k_ref):
        zero = jnp.zeros((C, C), BF)
        for sft in range(3):
            for r in range(2):
                rows = slice((r * 3 + sft) * C, (r * 3 + sft + 1) * C)
                for o in range(2):
                    columns = slice(o * C, (o + 1) * C)
                    tap = r - o
                    wlo[rows, columns] = k_ref[tap, sft] if tap >= 0 else zero
                    tap = r + 2 - o
                    whi[rows, columns] = k_ref[tap, sft] if tap <= 2 else zero

    def bcast_copy(k):
        return rc(band.at[k], band.at[k], bc_s.at[k], bc_r.at[k], nxt)

    def rs1_copy(grp, d):
        f = (f0 + d) % n
        return rc(
            rs1.at[grp, f], rs1_in.at[grp, f0], r1_s.at[grp, d], r1_r.at[grp, f0],
            (br, tile_of(f, g0)),
        )

    def rs1_wait(grp, d):
        f = (f0 + d) % n
        rc(
            rs1.at[grp, f], rs1_in.at[grp, f], r1_s.at[grp, d], r1_r.at[grp, f], (br, t)
        ).wait_recv()

    def rs2_copy(grp, d, s):
        g = (g0 + d) % n
        return rc(
            rs2.at[grp, g, s], rs2_in.at[half, g0, grp], r2_s.at[grp, d, s],
            r2_r.at[half, g0, grp], (2 * z + s, tile_of(f0, g)),
        )

    def gather2(d):
        g = (g0 + d) % n
        return rc(wall.at[g0], wall.at[g0], a2_s.at[d], a2_r.at[g0], (br, tile_of(f0, g)))

    def canvas_copy(k):
        return rc(canv.at[k], canv_in.at[k], cv_s.at[k], cv_r.at[k], prv)

    def entry_copy(k):
        return rc(canv.at[k], root_b.at[k], cv_s.at[k], rb_r.at[k], (last, t))

    def on_band(k):
        @pl.when(jnp.logical_not(is_root))
        def _():
            bcast_copy(k).wait_recv()

            @pl.when(pos < nz - 1)
            def _():
                bcast_copy(k).start()

        strips = jnp.dot(smat[...], band[k], preferred_element_type=F32).astype(BF)
        grp, kk = k // GROUP, k % GROUP
        rs1[grp, :, :, :, kk] = strips.reshape(n, n, 2, 16, C)

        @pl.when(kk == GROUP - 1)
        def _():
            for d in range(1, n):
                rs1_copy(grp, d).start()

    def on_rs1(grp):
        total = rs1[grp, f0]
        for d in range(1, n):
            rs1_wait(grp, d)
            total = total + rs1_in[grp, (f0 + d) % n]
        rs2[grp] = total
        for d in range(n):
            for s in (0, 1):
                if d:
                    rs2_copy(grp, d, s).start()
                else:

                    @pl.when(c != s)
                    def _(d=d, s=s):
                        rs2_copy(grp, d, s).start()

        rs2_in[half, g0, grp] = rs2[grp, g0, c]

    def on_gather1():
        for d in range(n):
            f = (f0 + d) % n
            for s in (0, 1):

                def wait(f=f, s=s):
                    rc(
                        win.at[0:HALF], wall.at[g0, f, s], a1_s.at[0, 0], a1_r.at[f, s], (br, t)
                    ).wait_recv()

                if d:
                    wait()
                else:
                    pl.when(c != s)(wait)
        for d in range(1, n):
            gather2(d).start()

    def on_gather2():
        for d in range(1, n):
            g = (g0 + d) % n
            rc(wall.at[g], wall.at[g], a2_s.at[d], a2_r.at[g], (br, t)).wait_recv()

    def on_canvas(k):
        w = wall[:, :, :, pl.ds(k, 1)].reshape(ops * 16, C)
        part = jnp.dot(pmat[...], w, preferred_element_type=F32)
        canv[k] = part.astype(BF)

        @pl.when(pos < nz - 1)
        def _():
            canvas_copy(k).wait_recv()
            canv[k] = (part + canv_in[k].astype(F32)).astype(BF)

        @pl.when(pos > 0)
        def _():
            canvas_copy(k).start()

        @pl.when(is_entry)
        def _():
            entry_copy(k).start()

    def event(cond, fun, *args):
        pl.when(cond)(lambda: fun(*args))

    def tick(tau, carry):
        k = tau - pos * HOP
        event(jnp.logical_and(k >= 0, k < HALF), on_band, jnp.clip(k, 0, HALF - 1))
        event(tau == GATHER1, on_gather1)
        event(tau == GATHER2, on_gather2)
        k = tau - (GATHER2 + (nz - 1 - pos) * HOP)
        event(jnp.logical_and(k >= 0, k < HALF), on_canvas, jnp.clip(k, 0, HALF - 1))
        for grp in range(GROUPS):
            event(tau == pos * HOP + grp * GROUP + GROUP - 1 + REDUCE, on_rs1, grp)
        return carry

    span = max(GATHER2, REDUCE) + (nz - 1) * HOP + HALF
    lax.fori_loop(0, span, tick, 0)

    def put(rows, lanes, value, width):
        m = value.reshape(-1, width, C)
        at = iota((1, width, 1), 1)
        before = jnp.where(at == 0, 0.0, pltpu.roll(m, 1, 1))
        after = jnp.where(at == width - 1, 0.0, pltpu.roll(m, width - 1, 1))
        for sft, v in enumerate((before, m, after)):
            zbuf[rows, lanes + sft * C : lanes + (sft + 1) * C] = v.reshape(-1, C).astype(BF)

    def conv_block(first, hi_first):
        lo = zbuf[pl.ds(first, 256)]
        hi = zbuf[pl.ds(hi_first, 256)]
        res = jnp.dot(lo, wlo[...], preferred_element_type=F32)
        res = res + jnp.dot(hi, whi[...], preferred_element_type=F32)
        return res.astype(BF)

    @pl.when(jnp.logical_not(is_root))
    def _():
        conv_weights(cl_ref)
        for hf in (0, 1):
            for g in range(n):
                for grp in range(GROUPS):

                    def wait(hf=hf, g=g, grp=grp):
                        rc(
                            rs2.at[grp, g, 0], rs2_in.at[hf, g, grp], r2_s.at[grp, 0, 0],
                            r2_r.at[hf, g, grp], (br, t),
                        ).wait_recv()

                    pl.when(jnp.logical_or(half != hf, g0 != g))(wait)
            total = rs2_in[hf, 0]
            for g in range(1, n):
                total = total + rs2_in[hf, g]
            crop[hf * HALF * 16 : (hf + 1) * HALF * 16] = total.reshape(HALF * 16, C)
        s1024 = iota((1024, 1), 0)
        target = band_row(s1024 // S) * 16 + (((s1024 % S) * ww) >> 6)
        lhs = jnp.where(iota((1, 256), 1) == target, 1.0, 0.0).astype(BF)
        cu[...] = jnp.dot(lhs, crop[...], preferred_element_type=F32).astype(BF).reshape(16, S, C)
        zbuf[0:S, 0 : 3 * C] = jnp.zeros((S, 3 * C), BF)
        zbuf[S // 2 * S : (S // 2 + 1) * S, 3 * C :] = jnp.zeros((S, 3 * C), BF)
        weight = ml_ref[...]

        def merge_block(b, carry):
            ups = []
            for i in range(8):
                r = (((b * 8 + i) * hh) >> 6) + top
                ups.append(cu[jnp.clip(r, 0, 15)])
            first = pl.multiple_of(b * 8 * S, 8 * S)
            both = jnp.concatenate(
                [x_ref[pl.ds(first, 8 * S)], jnp.concatenate(ups, axis=0)], axis=1
            )
            m = jnp.maximum(jnp.dot(both, weight, preferred_element_type=F32), 0.0)
            for i in range(8):
                pair = b * 4 + (i + 1) // 2
                rows = pl.ds(pl.multiple_of(pair * S, S), S)
                put(rows, 3 * C * ((i + 1) % 2), m[i * S : (i + 1) * S], S)
            return carry

        lax.fori_loop(0, S // 8, merge_block, 0)

        def conv_step(b, carry):
            first = pl.multiple_of(b * 256, 256)
            res = conv_block(first, pl.multiple_of(b * 256 + S, S))
            for i in range(4):
                for o in range(2):
                    at = pl.ds(pl.multiple_of(b * 512 + (2 * i + o) * S, S), S)
                    out_ref[at] = res[i * S : (i + 1) * S, o * C : (o + 1) * C]
            return carry

        lax.fori_loop(0, S // 8, conv_step, 0)

    def halo_copy(to_below):
        if to_below:
            peer = jnp.minimum(t + 1, tiles - 1)
            return rc(halo_out.at[1], halo.at[0], h_s.at[1], h_r.at[0], (last, peer))
        peer = jnp.maximum(t - 1, 0)
        return rc(halo_out.at[0], halo.at[1], h_s.at[0], h_r.at[1], (last, peer))

    def halo_wait(side):
        rc(halo_out.at[side], halo.at[side], h_s.at[side], h_r.at[side], (last, t)).wait_recv()

    @pl.when(is_root)
    def _():
        conv_weights(cg_ref)
        weight = mg_ref[...]

        def merge_row(r, pooled):
            both = jnp.concatenate([x_ref[r * GW : (r + 1) * GW], pooled], axis=1)
            m = jnp.maximum(jnp.dot(both, weight, preferred_element_type=F32), 0.0)
            pair = (r + 1) // 2
            put(slice(pair * GW, (pair + 1) * GW), 3 * C * ((r + 1) % 2), m, GW)
            return m

        def wait_entry(k):
            rc(canv.at[k], root_b.at[k], cv_s.at[k], rb_r.at[k], (last, t)).wait_recv()

        for k in range(HALF):
            m = merge_row(k, canv[k])
            if k == 0:
                halo_out[0] = m.astype(BF)
                pl.when(above)(lambda: halo_copy(False).start())
            wait_entry(k)
            m = merge_row(15 - k, root_b[k])
            if k == 0:
                halo_out[1] = m.astype(BF)
                pl.when(below)(lambda: halo_copy(True).start())

        zero = jnp.zeros((GW, 3 * C), BF)
        zbuf[0:GW, 0 : 3 * C] = zero
        zbuf[8 * GW : 9 * GW, 3 * C :] = zero

        @pl.when(above)
        def _():
            halo_wait(0)
            put(slice(0, GW), 0, halo[0].astype(F32), GW)

        @pl.when(below)
        def _():
            halo_wait(1)
            put(slice(8 * GW, 9 * GW), 3 * C, halo[1].astype(F32), GW)

        for q in range(8):
            res = conv_block(q * GW, (q + 1) * GW)
            for o in range(2):
                out_ref[(2 * q + o) * GW : (2 * q + o + 1) * GW] = res[:, o * C : (o + 1) * C]

    @pl.when(is_root)
    def _():
        for k in range(HALF):
            root_up(k).wait_send()
            root_side(k).wait_send()

    @pl.when(jnp.logical_and(jnp.logical_not(is_root), pos < nz - 1))
    def _():
        for k in range(HALF):
            bcast_copy(k).wait_send()

    for d in range(n):
        for core in (0, 1):

            def wait(d=d, core=core):
                gather1(d, core).wait_send()
                for grp in range(GROUPS):
                    rs2_copy(grp, d, core).wait_send()

            if d:
                wait()
            else:
                pl.when(c != core)(wait)
    for d in range(1, n):
        gather2(d).wait_send()
        for grp in range(GROUPS):
            rs1_copy(grp, d).wait_send()

    @pl.when(pos > 0)
    def _():
        for k in range(HALF):
            canvas_copy(k).wait_send()

    @pl.when(is_entry)
    def _():
        for k in range(HALF):
            entry_copy(k).wait_send()

    @pl.when(is_root)
    def _():
        for hf in (0, 1):
            for g in range(n):
                for grp in range(GROUPS):

                    def wait(hf=hf, g=g, grp=grp):
                        rc(
                            rs2.at[grp, g, 0], rs2_in.at[hf, g, grp], r2_s.at[grp, 0, 0],
                            r2_r.at[hf, g, grp], (br, t),
                        ).wait_recv()

                    pl.when(jnp.logical_or(half != hf, g0 != g))(wait)
        pl.when(above)(lambda: halo_copy(False).wait_send())
        pl.when(below)(lambda: halo_copy(True).wait_send())


def run(n, nz, features, merge_local, conv_local, merge_global, conv_global, offsets, sizes, owners):
    vm = functools.partial(pl.BlockSpec, memory_space=pltpu.VMEM)
    sm = functools.partial(pl.BlockSpec, memory_space=pltpu.SMEM)
    ops = 2 * n * n
    dma = pltpu.SemaphoreType.DMA
    out = pl.pallas_call(
        functools.partial(kernel, n, nz),
        out_shape=jax.ShapeDtypeStruct((CELLS, C), BF),
        in_specs=[vm()] * 5 + [sm()] * 3,
        out_specs=vm(),
        scratch_shapes=[
            pltpu.VMEM((16, 16, C), BF),
            pltpu.VMEM((n, n, 2, HALF, 16, C), BF),
            pltpu.VMEM((HALF, GW, C), BF),
            pltpu.VMEM((ops * 16, GW), BF),
            pltpu.VMEM((GW, ops * 16), BF),
            pltpu.VMEM((HALF, GW, C), BF),
            pltpu.VMEM((HALF, GW, C), BF),
            pltpu.VMEM((GROUPS, n, n, 2, GROUP, 16, C), BF),
            pltpu.VMEM((GROUPS, n, n, 2, GROUP, 16, C), BF),
            pltpu.VMEM((GROUPS, n, 2, GROUP, 16, C), BF),
            pltpu.VMEM((2, n, GROUPS, GROUP, 16, C), BF),
            pltpu.VMEM((HALF, GW, C), BF),
            pltpu.VMEM((2, GW, C), BF),
            pltpu.VMEM((2, GW, C), BF),
            pltpu.VMEM((256, C), BF),
            pltpu.VMEM((16, S, C), BF),
            pltpu.VMEM((9 * GW, 6 * C), BF),
            pltpu.VMEM((6 * C, 2 * C), BF),
            pltpu.VMEM((6 * C, 2 * C), BF),
            dma((HALF,)),
            dma((HALF,)),
            dma((HALF,)),
            dma((2, n)),
            dma((n, 2)),
            dma((n,)),
            dma((n,)),
            dma((HALF,)),
            dma((HALF,)),
            dma((HALF,)),
            dma((GROUPS, n)),
            dma((GROUPS, n)),
            dma((GROUPS, n, 2)),
            dma((2, n, GROUPS)),
            dma((2,)),
            dma((2,)),
        ],
        compiler_params=pltpu.CompilerParams(
            collective_id=0, has_side_effects=True, vmem_limit_bytes=48 * 1024 * 1024
        ),
        name="glue",
    )(
        features.reshape(CELLS, C), merge_local, conv_local, merge_global, conv_global,
        offsets, sizes, owners,
    )
    return out.reshape(features.shape)


def solution(mesh):
    nz = mesh.shape["branch"] // 2
    n = 1
    while n * n < mesh.shape["tile"]:
        n += 1
    in_specs = (P("branch", "tile", None, None, None), P(), P(), P(), P(), P(), P(), P())
    out_specs = P("branch", "tile", None, None, None)
    return jax.shard_map(
        functools.partial(run, n, nz),
        mesh=mesh,
        in_specs=in_specs,
        out_specs=out_specs,
        check_vma=False,
    )
```

time: 441 us -> 75.6 us (0.17); the launches traced: 434 us -> 75.2 us
  waiting for transfers between devices: 134 us -> 0 us
  other arithmetic: 95 us -> 0 us
  local copies, waits for them, and re-layouts: 92.8 us -> 6.67 us
  Pallas kernels: 0 us -> 68.5 us
  loops' own time: 58.1 us -> 0 us
  blocking collectives: 21.1 us -> 0 us
  between operations: 13.7 us -> 0.03 us
  starting transfers between devices: 11.2 us -> 0 us
  matrix products: 8.36 us -> 0 us
    psum x1 -> x0, waiting for transfers between devices: 116 us -> none  [shards(): summed = lax.psum(partial_band.astype(jnp.bfloat16), 'branch')]
    another operation x32 -> x0, other arithmetic: 88.6 us -> none
    pallas_call x0 -> x1, Pallas kernels: none -> 68.5 us  [run(): pl.pallas_call(functools.partial(kernel, n, nz), out_shape=jax.ShapeDtype...]
    another operation x2 -> x0, loops' own time: 58.1 us -> none  [the longest x1 58.1 us: shards(): lax.fori_loop(0, tile_count, visit, canvas_start)[:, :BAND_H, :GW]]
    scatter x16 -> x0, local copies, waits for them, and re-layouts: 46 us -> none  [place_one(): lax.dynamic_update_slice(canvas, current + window.astype(jnp.float32), (t...]
    all_to_all x1 -> x0, blocking collectives: 21.1 us -> none  [shards(): lax.all_to_all(requested, 'tile', split_axis=1, concat_axis=1, tiled=True)]
    all_to_all x1 -> x0, waiting for transfers between devices: 13.6 us -> none  [shards(): lax.all_to_all(outgoing, 'tile', split_axis=1, concat_axis=1, tiled=True)]
    dynamic_slice x18 -> x0, local copies, waits for them, and re-layouts: 10.8 us -> none  [the longest x16 9.4 us: visit(): slot_offsets[source, :, 1]]
  transfers between devices with their start and end apart: 4 -> 0, of which waited for: 3 -> 0; matrix products, arithmetic and copies ran while one was open for 1% -> 0% of each run, Pallas kernels for 0% -> 0%
where the time goes in v1:
time: 75.6 us; the launch traced here: 75.2 us
  Pallas kernels  68.5 us (91%)
  local copies, waits for them, and re-layouts  6.67 us (9%)
    pallas_call x1, Pallas kernels, run(): pl.pallas_call(functools.partial(kernel, n, nz), out_shape=jax.ShapeDtype...  68.5 us
    unnamed x14, local copies, waits for them, and re-layouts  6.67 us

profile of v1, /device:TPU:1, one launch (start us, length us, event | category | flops | bytes accessed | tf_op | source)
XLA Modules:
  0.0 75.2 jit_solution(227611824545207183)
XLA Ops:
  0.0 0.0 copy-start.1
  0.0 0.9 %copy.9.off_ref = s32[15,16,1,2]{3,2,1,0:T(1,128)S(1)} copy(s32[15,16,1,2]{1,3,2,0:T(2,128)} %param.13) | data formatting | bytes 3840 | tf_op args[5]
  0.9 0.9 %copy.10.size_ref = s32[15,16,1,2]{3,2,1,0:T(1,128)S(1)} copy(s32[15,16,1,2]{1,3,2,0:T(2,128)} %param.14) | data formatting | bytes 3840 | tf_op args[6]
  1.8 0.0 copy-start.3
  1.8 0.9 %copy.11.own_ref = s32[15,16,1]{2,1,0:T(8,128)S(1)} copy(s32[15,16,1]{1,2,0:T(1,128)} %param.15) | data formatting | bytes 1920 | tf_op args[7]
  2.7 0.0 copy-done.1
  2.7 0.0 copy-done.3
  2.7 0.0 copy-start
  2.7 1.2 %copy-done = bf16[1,1,1,4096,128]{4,3,2,1,0:T(8,128)(2,1)S(1)} copy-done((bf16[1,1,1,4096,128]{4,3,2,1,0:T(8,128)(2,1)S(1)}, bf16[1,1,1,4096,128]{4,3,2,1,0:T(8,128)(2,1)}, u32[]{:S(2)}) %copy-start) | copy-done | bytes 1048600
  3.9 0.0 copy-start.2
  3.9 1.0 %copy-done.2 = bf16[3,3,128,128]{3,2,1,0:T(8,128)(2,1)S(1)} copy-done((bf16[3,3,128,128]{3,2,1,0:T(8,128)(2,1)S(1)}, bf16[3,3,128,128]{3,2,1,0:T(8,128)(2,1)}, u32[]{:S(2)}) %copy-start.2) | copy-done | bytes 294936
  4.9 0.0 copy-start.4
  4.9 0.8 %copy-done.4 = bf16[256,128]{1,0:T(8,128)(2,1)S(1)} copy-done((bf16[256,128]{1,0:T(8,128)(2,1)S(1)}, bf16[256,128]{1,0:T(8,128)(2,1)}, u32[]{:S(2)}) %copy-start.4) | copy-done | bytes 65560
  5.7 68.5 %glue.1 = bf16[4096,128]{1,0:T(8,128)(2,1)S(1)} custom-call(bf16[4096,128]{1,0:T(8,128)(2,1)S(1)} %bitcast.3, bf16[256,128]{1,0:T(8,128)(2,1)S(1)} %copy-done.3, bf16[3,3,128,128]{3,2,1,0:T(8,128)(2,1)S(1)} %copy-done.1, bf16[256,128]{1,0:T(8,128)(2,1)S(1)} %copy-done.4, bf16[3,3,128,128]{3,2,1,0:T(8,128)(2,1)S(1)} %copy-done.2, ...), custom_call_target="tpu_custom_call" | custom-call | tf_op jit(solution)/shard_map/glue/pallas_call | solution.py:509
  74.3 1.0 %copy.13 = bf16[1,1,1,4096,128]{4,3,2,1,0:T(8,128)(2,1)} copy(bf16[1,1,1,4096,128]{4,3,2,1,0:T(8,128)(2,1)S(1)} %bitcast.2) | data formatting | bytes 2097152
Async XLA Ops:
  0.0 2.7 %copy-start.1 = (bf16[3,3,128,128]{3,2,1,0:T(8,128)(2,1)S(1)}, bf16[3,3,128,128]{3,2,1,0:T(8,128)(2,1)}, u32[]{:S(2)}) copy-start(bf16[3,3,128,128]{3,2,1,0:T(8,128)(2,1)} %cl_ref.1) | copy-start | bytes 884740
  1.8 0.9 %copy-start.3 = (bf16[256,128]{1,0:T(8,128)(2,1)S(1)}, bf16[256,128]{1,0:T(8,128)(2,1)}, u32[]{:S(2)}) copy-start(bf16[256,128]{1,0:T(8,128)(2,1)} %ml_ref.1) | copy-start | bytes 196612
  2.7 1.2 %copy-start = (bf16[1,1,1,4096,128]{4,3,2,1,0:T(8,128)(2,1)S(1)}, bf16[1,1,1,4096,128]{4,3,2,1,0:T(8,128)(2,1)}, u32[]{:S(2)}) copy-start(bf16[1,1,1,4096,128]{4,3,2,1,0:T(8,128)(2,1)} %param.8) | copy-start | bytes 3145732
  3.9 1.0 %copy-start.2 = (bf16[3,3,128,128]{3,2,1,0:T(8,128)(2,1)S(1)}, bf16[3,3,128,128]{3,2,1,0:T(8,128)(2,1)}, u32[]{:S(2)}) copy-start(bf16[3,3,128,128]{3,2,1,0:T(8,128)(2,1)} %cg_ref.1) | copy-start | bytes 884740
  4.9 0.8 %copy-start.4 = (bf16[256,128]{1,0:T(8,128)(2,1)S(1)}, bf16[256,128]{1,0:T(8,128)(2,1)}, u32[]{:S(2)}) copy-start(bf16[256,128]{1,0:T(8,128)(2,1)} %mg_ref.1) | copy-start | bytes 196612

commit v2 on v0

v2 whole, which is shorter than its diff:
```python
import functools

import jax
import jax.numpy as jnp
from jax import lax
from jax.experimental import pallas as pl
from jax.experimental.pallas import tpu as pltpu
from jax.sharding import PartitionSpec as P

MESH = pl.DeviceIdType.MESH
BF = jnp.bfloat16
F32 = jnp.float32
C = 128
S = 64
GW = 256
WIN = 16
CELLS = 4096
ROWS = 16
SLOTS = 15


def iota(shape, dim):
    return lax.broadcasted_iota(jnp.int32, shape, dim)


def kernel(
    n, x_hbm, ml_hbm, cl_hbm, mg_hbm, cg_hbm, off_hbm, size_hbm, own_hbm, out_ref,
    x_ref, ml_ref, mg_ref, conv_ref, off_ref, size_ref, own_ref,
    win, wall, grow, smat, pmat, rs1, rs1_in, rs2, rs2_in, rs3, crop, rows, mine, cu, zbuf, wlo, whi,
    in_s, gr_s, gr_r, zw_s, zw_r, a1_s, a1_r, a2_s, a2_r, r1_s, r1_r, r2_s, r2_r, zc_s, zc_r, m_s, m_r,
):
    tiles = n * n
    br = lax.axis_index("branch")
    t = lax.axis_index("tile")
    up = br % 2 == 1
    xx, yy = t // n, t % n
    f0 = jnp.where(up, xx, yy)
    g0 = jnp.where(up, yy, xx)
    last = ROWS - 1
    is_root = br == last
    is_local = br < last

    def tile_of(f, g):
        return jnp.where(up, f * n + g, g * n + f)

    def rc(src, dst, ss, rs, dev):
        return pltpu.make_async_remote_copy(
            src_ref=src, dst_ref=dst, send_sem=ss, recv_sem=rs, device_id=dev, device_id_type=MESH
        )

    barrier = pltpu.get_barrier_semaphore()

    def greet(b, tile):
        pl.semaphore_signal(barrier, inc=1, device_id=(b, tile), device_id_type=MESH)

    for d in range(1, ROWS):
        greet((br + d) % ROWS, t)
    for d in range(1, n):
        greet(br, ((xx + d) % n) * n + yy)
        greet(br, xx * n + (yy + d) % n)
    before = jnp.maximum(t - 1, 0)
    after = jnp.minimum(t + 1, tiles - 1)
    has_before, has_after = t > 0, t < tiles - 1
    is_first = br == 0
    first_up = jnp.logical_and(is_first, has_before)
    root_up = jnp.logical_and(is_root, has_before)
    root_down = jnp.logical_and(is_root, has_after)

    @pl.when(first_up)
    def _():
        greet(last, before)

    @pl.when(root_up)
    def _():
        greet(last, before)

    @pl.when(root_down)
    def _():
        greet(0, after)
        greet(last, after)

    def fetch(i, src, dst):
        return pltpu.make_async_copy(src, dst, in_s.at[i])

    fetches = [
        fetch(0, size_hbm, size_ref),
        fetch(1, off_hbm, off_ref),
        fetch(2, own_hbm, own_ref),
        fetch(3, x_hbm, x_ref),
        fetch(4, mg_hbm, mg_ref),
        fetch(5, ml_hbm, ml_ref),
    ]
    for f in fetches:
        f.start()
    pl.when(is_root)(lambda: fetch(6, cg_hbm, conv_ref).start())
    pl.when(is_local)(lambda: fetch(6, cl_hbm, conv_ref).start())
    for f in fetches[:4]:
        f.wait()

    slot = jnp.minimum(br, last - 1)
    top = off_ref[slot, 0, t]
    hh = size_ref[slot, 0, t]
    ww = size_ref[slot, 1, t]

    @pl.when(is_local)
    def _():
        sub = iota((256, 1), 0)
        sub_row = sub // WIN - top
        sub_col = sub % WIN
        lane64 = iota((1, 128), 1)
        inside = lane64 < S
        row_hits = jnp.where(jnp.logical_and(inside, ((lane64 * hh) >> 6) == sub_row), 1.0, 0.0)
        col_hits = jnp.where(jnp.logical_and(inside, ((lane64 * ww) >> 6) == sub_col), 1.0, 0.0)
        counts = jnp.sum(row_hits, axis=1, keepdims=True) * jnp.sum(col_hits, axis=1, keepdims=True)
        wide = 1024
        lane = iota((1, wide), 1)
        cols = jnp.where((((lane % S) * ww) >> 6) == sub_col, 1.0, 0.0)

        def pool_step(step, acc):
            rows_at = ((step * (wide // S) + lane // S) * hh) >> 6
            lhs = jnp.where(rows_at == sub_row, cols, 0.0).astype(BF)
            rhs = x_ref[pl.ds(pl.multiple_of(step * wide, wide), wide)]
            return acc + jnp.dot(lhs, rhs, preferred_element_type=F32)

        total = lax.fori_loop(0, CELLS // wide, pool_step, jnp.zeros((256, C), F32))
        win[...] = (total / jnp.maximum(counts, 1.0)).astype(BF).reshape(ROWS, WIN, C)

    count = ROWS - 1 + 2 * (n - 1)
    extra = jnp.where(first_up, 1, 0) + jnp.where(root_up, 1, 0) + jnp.where(root_down, 2, 0)
    pl.semaphore_wait(barrier, count + extra)

    def row_copy(r):
        return rc(x_ref.at[r * GW : (r + 1) * GW], grow, gr_s.at[r], gr_r.at[0], (r, t))

    far_first = (6, 7, 4, 8, 5, 9, 2, 10, 3, 11, 0, 12, 1, 13, 14)

    @pl.when(is_root)
    def _():
        for r in far_first:
            row_copy(r).start()
        grow[...] = x_ref[last * GW : (last + 1) * GW]

    def window_copy(d):
        r = (br + d) % ROWS
        odd = r % 2 == 1
        g, f = jnp.where(odd, yy, xx), jnp.where(odd, xx, yy)
        return rc(win.at[r], wall.at[g, f, br], zw_s.at[d], zw_r.at[br], (r, t))

    @pl.when(is_local)
    def _():
        for d in range(1, ROWS):
            window_copy(d).start()
        wall[g0, f0, slot] = win[br]

    diag = iota((WIN, GW), 1) - iota((WIN, GW), 0)

    def left_of(s, tile):
        return jnp.where(own_ref[s, 0, tile] == t, off_ref[s, 1, tile], -1024)

    def strip_step(i, carry):
        tile = tile_of(i // n, i % n)
        for s in range(SLOTS):
            at = pl.ds(pl.multiple_of((i * SLOTS + s) * WIN, WIN), WIN)
            smat[at] = jnp.where(diag == left_of(s, tile), 1.0, 0.0).astype(BF)
        return carry

    lax.fori_loop(0, tiles, strip_step, 0)

    piece = iota((1, GW), 1) // WIN
    place = iota((1, GW), 1) % WIN
    column = iota((GW, 1), 0)

    def place_step(i, carry):
        tile = tile_of(i % n, i // n)
        lefts = jnp.full((1, GW), -1024, jnp.int32)
        for s in range(SLOTS):
            lefts = jnp.where(piece == s, left_of(s, tile), lefts)
        pmat[i] = jnp.where(column == lefts + place, 1.0, 0.0).astype(BF)
        return carry

    def gather1(d):
        dev = (br, tile_of((f0 + d) % n, g0))
        own = wall.at[g0, f0, 0:SLOTS]
        return rc(own, own, a1_s.at[d], a1_r.at[f0], dev)

    def gather1_wait(d):
        f = (f0 + d) % n
        part = wall.at[g0, f, 0:SLOTS]
        rc(part, part, a1_s.at[d], a1_r.at[f], (br, t)).wait_recv()

    def gather2(d):
        dev = (br, tile_of(f0, (g0 + d) % n))
        own = wall.at[g0, :, 0:SLOTS]
        return rc(own, own, a2_s.at[d], a2_r.at[g0], dev)

    def gather2_wait(d):
        g = (g0 + d) % n
        part = wall.at[g, :, 0:SLOTS]
        rc(part, part, a2_s.at[d], a2_r.at[g], (br, t)).wait_recv()

    for s in range(SLOTS):

        @pl.when(br != s)
        def _(s=s):
            part = wall.at[g0, f0, s]
            rc(win.at[s], part, zw_s.at[s], zw_r.at[s], (br, t)).wait_recv()

    for d in range(1, n):
        gather1(d).start()

    @pl.when(is_local)
    def _():
        rc(grow, grow, gr_s.at[0], gr_r.at[0], (br, t)).wait_recv()

    def scatter1(d):
        f = (f0 + d) % n
        return rc(rs1.at[f], rs1_in.at[f0], r1_s.at[d], r1_r.at[f0], (br, tile_of(f, g0)))

    def scatter1_wait(d):
        f = (f0 + d) % n
        rc(rs1.at[f], rs1_in.at[f], r1_s.at[d], r1_r.at[f], (br, t)).wait_recv()

    block = n * SLOTS * WIN
    for d in [*range(1, n), 0]:
        f = (f0 + d) % n
        at = pl.ds(pl.multiple_of(f * block, WIN), block)
        strips = jnp.dot(smat[at], grow[...], preferred_element_type=F32).astype(BF)
        rs1[f] = strips.reshape(n, SLOTS, WIN, C)
        if d:
            scatter1(d).start()

    lax.fori_loop(0, tiles, place_step, 0)
    for i in range(n):
        for j in range(n):
            wall[i, j, SLOTS] = jnp.zeros((WIN, C), BF)

    for d in range(1, n):
        gather1_wait(d)
    for d in range(1, n):
        gather2(d).start()

    fetches[4].wait()
    fetches[5].wait()
    fetch(6, cl_hbm, conv_ref).wait()
    zero = jnp.zeros((C, C), BF)
    for sft in range(3):
        for r in range(2):
            at = slice((r * 3 + sft) * C, (r * 3 + sft + 1) * C)
            for o in range(2):
                to = slice(o * C, (o + 1) * C)
                tap = r - o
                wlo[at, to] = conv_ref[tap, sft] if tap >= 0 else zero
                tap = r + 2 - o
                whi[at, to] = conv_ref[tap, sft] if tap <= 2 else zero

    def scatter2(d):
        g = (g0 + d) % n
        return rc(rs2.at[g], rs2_in.at[g0], r2_s.at[d], r2_r.at[g0], (br, tile_of(f0, g)))

    def scatter2_wait(d):
        g = (g0 + d) % n
        rc(rs2.at[g], rs2_in.at[g], r2_s.at[d], r2_r.at[g], (br, t)).wait_recv()

    for d in range(1, n):
        scatter1_wait(d)
    for d in [*range(1, n), 0]:
        g = (g0 + d) % n
        total = rs1[f0, g]
        for e in range(1, n):
            total = total + rs1_in[(f0 + e) % n, g]
        rs2[g] = total
        if d:
            scatter2(d).start()

    def merged_copy():
        return rc(mine, rows.at[br + 1], m_s.at[0], m_r.at[br + 1], (last, t))

    def edge_up():
        return rc(mine, rows.at[ROWS + 1], m_s.at[1], m_r.at[ROWS + 1], (last, before))

    def edge_down():
        return rc(mine, rows.at[0], m_s.at[1], m_r.at[0], (last, after))

    for d in range(1, n):
        gather2_wait(d)
    pooled = jnp.zeros((GW, C), F32)
    for i in range(n):
        for j in range(n):
            w = wall[i, j].reshape(GW, C)
            pooled = pooled + jnp.dot(pmat[i * n + j], w, preferred_element_type=F32)
    both = jnp.concatenate([grow[...], pooled.astype(BF)], axis=1)
    merged = jnp.maximum(jnp.dot(both, mg_ref[...], preferred_element_type=F32), 0.0)
    mine[...] = merged.astype(BF)
    pl.when(is_local)(lambda: merged_copy().start())
    pl.when(first_up)(lambda: edge_up().start())
    pl.when(root_down)(lambda: edge_down().start())

    def crop_copy(d):
        b = (br + d) % ROWS
        return rc(rs3.at[b], crop.at[br], zc_s.at[d], zc_r.at[br], (b, t))

    for d in range(1, n):
        scatter2_wait(d)
    total = rs2[g0]
    for d in range(1, n):
        total = total + rs2_in[(g0 + d) % n]
    rs3[0:SLOTS] = total
    for d in range(1, ROWS):

        @pl.when((br + d) % ROWS != last)
        def _(d=d):
            crop_copy(d).start()

    def put(at, lanes, value, width):
        m = value.reshape(-1, width, C)
        col = iota((1, width, 1), 1)
        left = jnp.where(col == 0, 0.0, pltpu.roll(m, 1, 1))
        right = jnp.where(col == width - 1, 0.0, pltpu.roll(m, width - 1, 1))
        for sft, v in enumerate((left, m, right)):
            zbuf[at, lanes + sft * C : lanes + (sft + 1) * C] = v.reshape(-1, C).astype(BF)

    def conv_block(first, hi_first):
        lo = zbuf[pl.ds(first, 256)]
        hi = zbuf[pl.ds(hi_first, 256)]
        res = jnp.dot(lo, wlo[...], preferred_element_type=F32)
        res = res + jnp.dot(hi, whi[...], preferred_element_type=F32)
        return res.astype(BF)

    @pl.when(is_local)
    def _():
        zbuf[0:S, 0 : 3 * C] = jnp.zeros((S, 3 * C), BF)
        zbuf[S // 2 * S : (S // 2 + 1) * S, 3 * C :] = jnp.zeros((S, 3 * C), BF)
        s1024 = iota((1024, 1), 0)
        target = (s1024 // S) * WIN + (((s1024 % S) * ww) >> 6)
        lhs = jnp.where(iota((1, 256), 1) == target, 1.0, 0.0).astype(BF)
        weight = ml_ref[...]
        crop[br] = rs3[slot]
        for r in range(ROWS):

            @pl.when(br != r)
            def _(r=r):
                rc(rs3.at[0], crop.at[r], zc_s.at[r], zc_r.at[r], (br, t)).wait_recv()

        strips = crop[...].reshape(ROWS * WIN, C)
        cu[...] = jnp.dot(lhs, strips, preferred_element_type=F32).astype(BF).reshape(ROWS, S, C)

        def merge_block(b, carry):
            ups = []
            for i in range(8):
                r = (((b * 8 + i) * hh) >> 6) + top
                ups.append(cu[jnp.clip(r, 0, ROWS - 1)])
            first = pl.multiple_of(b * 8 * S, 8 * S)
            both = jnp.concatenate(
                [x_ref[pl.ds(first, 8 * S)], jnp.concatenate(ups, axis=0)], axis=1
            )
            m = jnp.maximum(jnp.dot(both, weight, preferred_element_type=F32), 0.0)
            for i in range(8):
                pair = b * 4 + (i + 1) // 2
                at = pl.ds(pl.multiple_of(pair * S, S), S)
                put(at, 3 * C * ((i + 1) % 2), m[i * S : (i + 1) * S], S)
            return carry

        lax.fori_loop(0, S // 8, merge_block, 0)

        def conv_step(b, carry):
            first = pl.multiple_of(b * 256, 256)
            res = conv_block(first, pl.multiple_of(b * 256 + S, S))
            for i in range(4):
                for o in range(2):
                    at = pl.ds(pl.multiple_of(b * 512 + (2 * i + o) * S, S), S)
                    out_ref[at] = res[i * S : (i + 1) * S, o * C : (o + 1) * C]
            return carry

        lax.fori_loop(0, S // 8, conv_step, 0)

    @pl.when(is_root)
    def _():
        rows[ROWS] = mine[...]

        @pl.when(jnp.logical_not(has_before))
        def _():
            rows[0] = jnp.zeros((GW, C), BF)

        @pl.when(jnp.logical_not(has_after))
        def _():
            rows[ROWS + 1] = jnp.zeros((GW, C), BF)

        def wait(i):
            rc(mine, rows.at[i], m_s.at[0], m_r.at[i], (br, t)).wait_recv()

        here = set()
        done = set()
        for i in (16, 15, 1, 2, 13, 14, 3, 4, 11, 12, 5, 6, 9, 10, 0, 17, 7, 8):
            if i == 0:
                pl.when(has_before)(functools.partial(wait, 0))
            elif i == ROWS + 1:
                pl.when(has_after)(functools.partial(wait, ROWS + 1))
            elif i != ROWS:
                wait(i)
            put(slice(i // 2 * GW, (i // 2 + 1) * GW), 3 * C * (i % 2), rows[i].astype(F32), GW)
            here.add(i)
            for q in range(8):
                if q not in done and here >= {2 * q, 2 * q + 1, 2 * q + 2, 2 * q + 3}:
                    done.add(q)
                    res = conv_block(q * GW, (q + 1) * GW)
                    for o in range(2):
                        at = slice((2 * q + o) * GW, (2 * q + o + 1) * GW)
                        out_ref[at] = res[:, o * C : (o + 1) * C]

    @pl.when(is_root)
    def _():
        for r in far_first:
            row_copy(r).wait_send()

    @pl.when(is_local)
    def _():
        for d in range(1, ROWS):
            window_copy(d).wait_send()
        merged_copy().wait_send()

    for d in range(1, n):
        gather1(d).wait_send()
        gather2(d).wait_send()
        scatter1(d).wait_send()
        scatter2(d).wait_send()
    for d in range(1, ROWS):

        @pl.when((br + d) % ROWS != last)
        def _(d=d):
            crop_copy(d).wait_send()

    pl.when(first_up)(lambda: edge_up().wait_send())
    pl.when(root_down)(lambda: edge_down().wait_send())


def run(n, features, merge_local, conv_local, merge_global, conv_global, offsets, sizes, owners):
    hbm = pl.BlockSpec(memory_space=pltpu.HBM)
    dma = pltpu.SemaphoreType.DMA

    def vm(*shape):
        return pltpu.VMEM(shape, BF)

    def sm(*shape):
        return pltpu.SMEM(shape, jnp.int32)

    tiles = n * n
    out = pl.pallas_call(
        functools.partial(kernel, n),
        out_shape=jax.ShapeDtypeStruct((CELLS, C), BF),
        in_specs=[hbm] * 8,
        out_specs=pl.BlockSpec(memory_space=pltpu.VMEM),
        scratch_shapes=[
            vm(CELLS, C),
            vm(2 * C, C),
            vm(2 * C, C),
            vm(3, 3, C, C),
            sm(SLOTS, 2, tiles),
            sm(SLOTS, 2, tiles),
            sm(SLOTS, 1, tiles),
            vm(ROWS, WIN, C),
            vm(n, n, ROWS, WIN, C),
            vm(GW, C),
            vm(tiles * SLOTS * WIN, GW),
            vm(tiles, GW, GW),
            vm(n, n, SLOTS, WIN, C),
            vm(n, n, SLOTS, WIN, C),
            vm(n, SLOTS, WIN, C),
            vm(n, SLOTS, WIN, C),
            vm(ROWS, WIN, C),
            vm(ROWS, WIN, C),
            vm(ROWS + 2, GW, C),
            vm(GW, C),
            vm(ROWS, S, C),
            vm(9 * GW, 6 * C),
            vm(6 * C, 2 * C),
            vm(6 * C, 2 * C),
            dma((7,)),
            dma((ROWS,)),
            dma((1,)),
            dma((ROWS,)),
            dma((ROWS,)),
            dma((n,)),
            dma((n,)),
            dma((n,)),
            dma((n,)),
            dma((n,)),
            dma((n,)),
            dma((n,)),
            dma((n,)),
            dma((ROWS,)),
            dma((ROWS,)),
            dma((2,)),
            dma((ROWS + 2,)),
        ],
        compiler_params=pltpu.CompilerParams(
            collective_id=0, has_side_effects=True, vmem_limit_bytes=58 * 1024 * 1024
        ),
        name="glue",
    )(
        features.reshape(CELLS, C), merge_local, conv_local, merge_global, conv_global,
        offsets.transpose(0, 2, 3, 1).reshape(SLOTS, 2, tiles),
        sizes.transpose(0, 2, 3, 1).reshape(SLOTS, 2, tiles),
        owners.transpose(0, 2, 1),
    )
    return out.reshape(features.shape)


def solution(mesh):
    n = 1
    while n * n < mesh.shape["tile"]:
        n += 1
    in_specs = (P("branch", "tile", None, None, None), P(), P(), P(), P(), P(), P(), P())
    out_specs = P("branch", "tile", None, None, None)
    return jax.shard_map(
        functools.partial(run, n),
        mesh=mesh,
        in_specs=in_specs,
        out_specs=out_specs,
        check_vma=False,
    )
```

time: 441 us -> 52.5 us (0.12); the launches traced: 434 us -> 52.3 us
  waiting for transfers between devices: 134 us -> 0 us
  other arithmetic: 95 us -> 0 us
  local copies, waits for them, and re-layouts: 92.8 us -> 2.26 us
  loops' own time: 58.1 us -> 0 us
  Pallas kernels: 0 us -> 50.1 us
  blocking collectives: 21.1 us -> 0 us
  between operations: 13.7 us -> 0.01 us
  starting transfers between devices: 11.2 us -> 0 us
  matrix products: 8.36 us -> 0 us
    psum x1 -> x0, waiting for transfers between devices: 116 us -> none  [shards(): summed = lax.psum(partial_band.astype(jnp.bfloat16), 'branch')]
    another operation x32 -> x0, other arithmetic: 88.6 us -> none
    another operation x2 -> x0, loops' own time: 58.1 us -> none  [the longest x1 58.1 us: shards(): lax.fori_loop(0, tile_count, visit, canvas_start)[:, :BAND_H, :GW]]
    pallas_call x0 -> x1, Pallas kernels: none -> 50.1 us  [run(): pl.pallas_call(functools.partial(kernel, n), out_shape=jax.ShapeDtypeStru...]
    scatter x16 -> x0, local copies, waits for them, and re-layouts: 46 us -> none  [place_one(): lax.dynamic_update_slice(canvas, current + window.astype(jnp.float32), (t...]
    all_to_all x1 -> x0, blocking collectives: 21.1 us -> none  [shards(): lax.all_to_all(requested, 'tile', split_axis=1, concat_axis=1, tiled=True)]
    all_to_all x1 -> x0, waiting for transfers between devices: 13.6 us -> none  [shards(): lax.all_to_all(outgoing, 'tile', split_axis=1, concat_axis=1, tiled=True)]
    dynamic_slice x18 -> x0, local copies, waits for them, and re-layouts: 10.8 us -> none  [the longest x16 9.4 us: visit(): slot_offsets[source, :, 1]]
  transfers between devices with their start and end apart: 4 -> 0, of which waited for: 3 -> 0; matrix products, arithmetic and copies ran while one was open for 1% -> 0% of each run, Pallas kernels for 0% -> 0%
where the time goes in v2:
time: 52.5 us; the launch traced here: 52.3 us
  Pallas kernels  50.1 us (95%)
  local copies, waits for them, and re-layouts  2.26 us (4%)
    pallas_call x1, Pallas kernels, run(): pl.pallas_call(functools.partial(kernel, n), out_shape=jax.ShapeDtypeStru...  50.1 us
    unnamed x1, local copies, waits for them, and re-layouts  2.26 us

profile of v2, /device:TPU:1, one launch (start us, length us, event | category | flops | bytes accessed | tf_op | source)
XLA Modules:
  0.0 52.3 jit_solution(5635958026013066158)
XLA Ops:
  0.0 50.1 %glue.1 = bf16[4096,128]{1,0:T(8,128)(2,1)} custom-call(bf16[4096,128]{1,0:T(8,128)(2,1)} %bitcast.14, bf16[256,128]{1,0:T(8,128)(2,1)} %ml_hbm.1, bf16[3,3,128,128]{3,2,1,0:T(8,128)(2,1)} %cl_hbm.1, bf16[256,128]{1,0:T(8,128)(2,1)} %mg_hbm.1, bf16[3,3,128,128]{3,2,1,0:T(8,128)(2,1)} %cg_hbm.1, s32[15,2,16]{2,1,0:T(2,128)} %bitcast.15, ...), custom_call_target="tpu_custom_call" | custom-call | tf_op jit(solution)/shard_map/glue/pallas_call | solution.py:447
  50.1 2.3 %copy.12 = bf16[1,1,1,4096,128]{4,3,2,1,0:T(8,128)(2,1)} copy(bf16[1,1,1,4096,128]{4,3,2,1,0:T(8,128)(2,1)} %bitcast.13) | data formatting | bytes 2097152

commit v3 on v2

--- a/solution.py
+++ b/solution.py
@@ -26,7 +26,7 @@
 def kernel(
     n, x_hbm, ml_hbm, cl_hbm, mg_hbm, cg_hbm, off_hbm, size_hbm, own_hbm, out_ref,
     x_ref, ml_ref, mg_ref, conv_ref, off_ref, size_ref, own_ref,
-    win, wall, grow, smat, pmat, rs1, rs1_in, rs2, rs2_in, rs3, crop, rows, mine, cu, zbuf, wlo, whi,
+    win, wall, bands, smat, pmat, strip, strip_in, canv, canv_in, total_strip, crop, rows, mine, cu, zbuf, wlo, whi,
     in_s, gr_s, gr_r, zw_s, zw_r, a1_s, a1_r, a2_s, a2_r, r1_s, r1_r, r2_s, r2_r, zc_s, zc_r, m_s, m_r,
 ):
     tiles = n * n
@@ -130,7 +130,8 @@
     pl.semaphore_wait(barrier, count + extra)
 
     def row_copy(r):
-        return rc(x_ref.at[r * GW : (r + 1) * GW], grow, gr_s.at[r], gr_r.at[0], (r, t))
+        f = xx if r % 2 else yy
+        return rc(x_ref.at[r * GW : (r + 1) * GW], bands.at[f], gr_s.at[r], gr_r.at[0], (r, t))
 
     far_first = (6, 7, 4, 8, 5, 9, 2, 10, 3, 11, 0, 12, 1, 13, 14)
 
@@ -138,106 +139,86 @@
     def _():
         for r in far_first:
             row_copy(r).start()
-        grow[...] = x_ref[last * GW : (last + 1) * GW]
+        bands[f0] = x_ref[last * GW : (last + 1) * GW]
 
     def window_copy(d):
         r = (br + d) % ROWS
-        odd = r % 2 == 1
-        g, f = jnp.where(odd, yy, xx), jnp.where(odd, xx, yy)
-        return rc(win.at[r], wall.at[g, f, br], zw_s.at[d], zw_r.at[br], (r, t))
+        f = jnp.where(r % 2 == 1, xx, yy)
+        return rc(win.at[r], wall.at[f, br], zw_s.at[d], zw_r.at[br], (r, t))
 
     @pl.when(is_local)
     def _():
         for d in range(1, ROWS):
             window_copy(d).start()
-        wall[g0, f0, slot] = win[br]
-
-    diag = iota((WIN, GW), 1) - iota((WIN, GW), 0)
-
-    def left_of(s, tile):
-        return jnp.where(own_ref[s, 0, tile] == t, off_ref[s, 1, tile], -1024)
-
-    def strip_step(i, carry):
-        tile = tile_of(i // n, i % n)
+        wall[f0, slot] = win[br]
+
+    def axes_of(tile):
+        high, low = lax.div(tile, n), lax.rem(tile, n)
+        return jnp.where(up, high, low), jnp.where(up, low, high)
+
+    diag = iota((WIN, n * GW), 1) - iota((WIN, n * GW), 0)
+
+    def strip_step(g, carry):
+        tile = tile_of(f0, g)
         for s in range(SLOTS):
-            at = pl.ds(pl.multiple_of((i * SLOTS + s) * WIN, WIN), WIN)
-            smat[at] = jnp.where(diag == left_of(s, tile), 1.0, 0.0).astype(BF)
+            f_own, g_own = axes_of(own_ref[s, 0, tile])
+            target = jnp.where(g_own == g0, f_own * GW + off_ref[s, 1, tile], -(n + 1) * GW)
+            at = pl.ds(pl.multiple_of((g * SLOTS + s) * WIN, WIN), WIN)
+            smat[at] = jnp.where(diag == target, 1.0, 0.0).astype(BF)
         return carry
-
-    lax.fori_loop(0, tiles, strip_step, 0)
 
     piece = iota((1, GW), 1) // WIN
     place = iota((1, GW), 1) % WIN
     column = iota((GW, 1), 0)
 
-    def place_step(i, carry):
-        tile = tile_of(i % n, i // n)
-        lefts = jnp.full((1, GW), -1024, jnp.int32)
+    def place_step(f, carry):
+        tile = tile_of(f, g0)
+        target = jnp.full((1, GW), -(n + 1) * GW, jnp.int32)
         for s in range(SLOTS):
-            lefts = jnp.where(piece == s, left_of(s, tile), lefts)
-        pmat[i] = jnp.where(column == lefts + place, 1.0, 0.0).astype(BF)
+            f_own, g_own = axes_of(own_ref[s, 0, tile])
+            here = jnp.where(f_own == f0, g_own * GW + off_ref[s, 1, tile], -(n + 1) * GW)
+            target = jnp.where(piece == s, here, target)
+        target = target + place
+        for g in range(n):
+            pmat[g, f] = jnp.where(column + g * GW == target, 1.0, 0.0).astype(BF)
+        wall[f, SLOTS] = jnp.zeros((WIN, C), BF)
         return carry
 
-    def gather1(d):
-        dev = (br, tile_of((f0 + d) % n, g0))
-        own = wall.at[g0, f0, 0:SLOTS]
-        return rc(own, own, a1_s.at[d], a1_r.at[f0], dev)
-
-    def gather1_wait(d):
+    lax.fori_loop(0, n, place_step, 0)
+    lax.fori_loop(0, n, strip_step, 0)
+
+    def gather_windows(d):
+        own = wall.at[f0, 0:SLOTS]
+        return rc(own, own, a1_s.at[d], a1_r.at[f0], (br, tile_of((f0 + d) % n, g0)))
+
+    def gather_windows_wait(d):
         f = (f0 + d) % n
-        part = wall.at[g0, f, 0:SLOTS]
+        part = wall.at[f, 0:SLOTS]
         rc(part, part, a1_s.at[d], a1_r.at[f], (br, t)).wait_recv()
 
-    def gather2(d):
-        dev = (br, tile_of(f0, (g0 + d) % n))
-        own = wall.at[g0, :, 0:SLOTS]
-        return rc(own, own, a2_s.at[d], a2_r.at[g0], dev)
-
-    def gather2_wait(d):
-        g = (g0 + d) % n
-        part = wall.at[g, :, 0:SLOTS]
-        rc(part, part, a2_s.at[d], a2_r.at[g], (br, t)).wait_recv()
+    def gather_bands(d):
+        own = bands.at[f0]
+        return rc(own, own, r1_s.at[d], r1_r.at[f0], (br, tile_of((f0 + d) % n, g0)))
+
+    def gather_bands_wait(d):
+        f = (f0 + d) % n
+        rc(bands.at[f], bands.at[f], r1_s.at[d], r1_r.at[f], (br, t)).wait_recv()
 
     for s in range(SLOTS):
 
         @pl.when(br != s)
         def _(s=s):
-            part = wall.at[g0, f0, s]
-            rc(win.at[s], part, zw_s.at[s], zw_r.at[s], (br, t)).wait_recv()
-
-    for d in range(1, n):
-        gather1(d).start()
+            rc(win.at[s], wall.at[f0, s], zw_s.at[s], zw_r.at[s], (br, t)).wait_recv()
+
+    for d in range(1, n):
+        gather_windows(d).start()
 
     @pl.when(is_local)
     def _():
-        rc(grow, grow, gr_s.at[0], gr_r.at[0], (br, t)).wait_recv()
-
-    def scatter1(d):
-        f = (f0 + d) % n
-        return rc(rs1.at[f], rs1_in.at[f0], r1_s.at[d], r1_r.at[f0], (br, tile_of(f, g0)))
-
-    def scatter1_wait(d):
-        f = (f0 + d) % n
-        rc(rs1.at[f], rs1_in.at[f], r1_s.at[d], r1_r.at[f], (br, t)).wait_recv()
-
-    block = n * SLOTS * WIN
-    for d in [*range(1, n), 0]:
-        f = (f0 + d) % n
-        at = pl.ds(pl.multiple_of(f * block, WIN), block)
-        strips = jnp.dot(smat[at], grow[...], preferred_element_type=F32).astype(BF)
-        rs1[f] = strips.reshape(n, SLOTS, WIN, C)
-        if d:
-            scatter1(d).start()
-
-    lax.fori_loop(0, tiles, place_step, 0)
-    for i in range(n):
-        for j in range(n):
-            wall[i, j, SLOTS] = jnp.zeros((WIN, C), BF)
-
-    for d in range(1, n):
-        gather1_wait(d)
-    for d in range(1, n):
-        gather2(d).start()
+        rc(bands.at[0], bands.at[f0], gr_s.at[0], gr_r.at[0], (br, t)).wait_recv()
+
+    for d in range(1, n):
+        gather_bands(d).start()
 
     fetches[4].wait()
     fetches[5].wait()
@@ -253,24 +234,47 @@
                 tap = r + 2 - o
                 whi[at, to] = conv_ref[tap, sft] if tap <= 2 else zero
 
-    def scatter2(d):
+    def scatter_canvas(d):
         g = (g0 + d) % n
-        return rc(rs2.at[g], rs2_in.at[g0], r2_s.at[d], r2_r.at[g0], (br, tile_of(f0, g)))
-
-    def scatter2_wait(d):
+        return rc(canv.at[g], canv_in.at[g0], a2_s.at[d], a2_r.at[g0], (br, tile_of(f0, g)))
+
+    def scatter_canvas_wait(d):
         g = (g0 + d) % n
-        rc(rs2.at[g], rs2_in.at[g], r2_s.at[d], r2_r.at[g], (br, t)).wait_recv()
-
-    for d in range(1, n):
-        scatter1_wait(d)
+        rc(canv.at[g], canv_in.at[g], a2_s.at[d], a2_r.at[g], (br, t)).wait_recv()
+
+    def scatter_strips(d):
+        g = (g0 + d) % n
+        return rc(strip.at[g], strip_in.at[g0], r2_s.at[d], r2_r.at[g0], (br, tile_of(f0, g)))
+
+    def scatter_strips_wait(d):
+        g = (g0 + d) % n
+        rc(strip.at[g], strip_in.at[g], r2_s.at[d], r2_r.at[g], (br, t)).wait_recv()
+
+    for d in range(1, n):
+        gather_windows_wait(d)
+    pooled = jnp.zeros((GW, C), F32)
     for d in [*range(1, n), 0]:
         g = (g0 + d) % n
-        total = rs1[f0, g]
-        for e in range(1, n):
-            total = total + rs1_in[(f0 + e) % n, g]
-        rs2[g] = total
+        pooled = jnp.zeros((GW, C), F32)
+        for f in range(n):
+            w = wall[f].reshape(GW, C)
+            pooled = pooled + jnp.dot(pmat[g, f], w, preferred_element_type=F32)
         if d:
-            scatter2(d).start()
+            canv[g] = pooled.astype(BF)
+            scatter_canvas(d).start()
+
+    for d in range(1, n):
+        gather_bands_wait(d)
+    own_strips = None
+    block = SLOTS * WIN
+    for d in [*range(1, n), 0]:
+        g = (g0 + d) % n
+        at = pl.ds(pl.multiple_of(g * block, WIN), block)
+        cut = jnp.dot(smat[at], bands[...].reshape(n * GW, C), preferred_element_type=F32)
+        own_strips = cut.astype(BF).reshape(SLOTS, WIN, C)
+        if d:
+            strip[g] = own_strips
+            scatter_strips(d).start()
 
     def merged_copy():
         return rc(mine, rows.at[br + 1], m_s.at[0], m_r.at[br + 1], (last, t))
@@ -282,13 +286,9 @@
         return rc(mine, rows.at[0], m_s.at[1], m_r.at[0], (last, after))
 
     for d in range(1, n):
-        gather2_wait(d)
-    pooled = jnp.zeros((GW, C), F32)
-    for i in range(n):
-        for j in range(n):
-            w = wall[i, j].reshape(GW, C)
-            pooled = pooled + jnp.dot(pmat[i * n + j], w, preferred_element_type=F32)
-    both = jnp.concatenate([grow[...], pooled.astype(BF)], axis=1)
+        scatter_canvas_wait(d)
+        pooled = pooled + canv_in[(g0 + d) % n].astype(F32)
+    both = jnp.concatenate([bands[f0], pooled.astype(BF)], axis=1)
     merged = jnp.maximum(jnp.dot(both, mg_ref[...], preferred_element_type=F32), 0.0)
     mine[...] = merged.astype(BF)
     pl.when(is_local)(lambda: merged_copy().start())
@@ -297,14 +297,12 @@
 
     def crop_copy(d):
         b = (br + d) % ROWS
-        return rc(rs3.at[b], crop.at[br], zc_s.at[d], zc_r.at[br], (b, t))
-
-    for d in range(1, n):
-        scatter2_wait(d)
-    total = rs2[g0]
-    for d in range(1, n):
-        total = total + rs2_in[(g0 + d) % n]
-    rs3[0:SLOTS] = total
+        return rc(total_strip.at[b], crop.at[br], zc_s.at[d], zc_r.at[br], (b, t))
+
+    for d in range(1, n):
+        scatter_strips_wait(d)
+        own_strips = own_strips + strip_in[(g0 + d) % n]
+    total_strip[0:SLOTS] = own_strips
     for d in range(1, ROWS):
 
         @pl.when((br + d) % ROWS != last)
@@ -334,12 +332,12 @@
         target = (s1024 // S) * WIN + (((s1024 % S) * ww) >> 6)
         lhs = jnp.where(iota((1, 256), 1) == target, 1.0, 0.0).astype(BF)
         weight = ml_ref[...]
-        crop[br] = rs3[slot]
+        crop[br] = total_strip[slot]
         for r in range(ROWS):
 
             @pl.when(br != r)
             def _(r=r):
-                rc(rs3.at[0], crop.at[r], zc_s.at[r], zc_r.at[r], (br, t)).wait_recv()
+                rc(total_strip.at[0], crop.at[r], zc_s.at[r], zc_r.at[r], (br, t)).wait_recv()
 
         strips = crop[...].reshape(ROWS * WIN, C)
         cu[...] = jnp.dot(lhs, strips, preferred_element_type=F32).astype(BF).reshape(ROWS, S, C)
@@ -419,10 +417,10 @@
         merged_copy().wait_send()
 
     for d in range(1, n):
-        gather1(d).wait_send()
-        gather2(d).wait_send()
-        scatter1(d).wait_send()
-        scatter2(d).wait_send()
+        gather_windows(d).wait_send()
+        gather_bands(d).wait_send()
+        scatter_canvas(d).wait_send()
+        scatter_strips(d).wait_send()
     for d in range(1, ROWS):
 
         @pl.when((br + d) % ROWS != last)
@@ -458,14 +456,14 @@
             sm(SLOTS, 2, tiles),
             sm(SLOTS, 1, tiles),
             vm(ROWS, WIN, C),
-            vm(n, n, ROWS, WIN, C),
-            vm(GW, C),
-            vm(tiles * SLOTS * WIN, GW),
-            vm(tiles, GW, GW),
-            vm(n, n, SLOTS, WIN, C),
-            vm(n, n, SLOTS, WIN, C),
+            vm(n, ROWS, WIN, C),
+            vm(n, GW, C),
+            vm(n * SLOTS * WIN, n * GW),
+            vm(n, n, GW, GW),
             vm(n, SLOTS, WIN, C),
             vm(n, SLOTS, WIN, C),
+            vm(n, GW, C),
+            vm(n, GW, C),
             vm(ROWS, WIN, C),
             vm(ROWS, WIN, C),
             vm(ROWS + 2, GW, C),

time: 52.5 us -> 44.9 us (0.86)
  Pallas kernels: 50.1 us -> 42.5 us
    pallas_call x1, Pallas kernels: 50.1 us -> 42.5 us  [run(): pl.pallas_call(functools.partial(kernel, n), out_shape=jax.ShapeDtypeStru...]
where the time goes in v3:
time: 44.9 us; the launch traced here: 44.8 us
  Pallas kernels  42.5 us (95%)
  local copies, waits for them, and re-layouts  2.26 us (5%)
    pallas_call x1, Pallas kernels, run(): pl.pallas_call(functools.partial(kernel, n), out_shape=jax.ShapeDtypeStru...  42.5 us
    unnamed x1, local copies, waits for them, and re-layouts  2.26 us

profile of v3, /device:TPU:1, one launch (start us, length us, event | category | flops | bytes accessed | tf_op | source)
XLA Modules:
  0.0 44.8 jit_solution(5248947191976066911)
XLA Ops:
  0.0 42.5 %glue.1 = bf16[4096,128]{1,0:T(8,128)(2,1)} custom-call(bf16[4096,128]{1,0:T(8,128)(2,1)} %bitcast.14, bf16[256,128]{1,0:T(8,128)(2,1)} %ml_hbm.1, bf16[3,3,128,128]{3,2,1,0:T(8,128)(2,1)} %cl_hbm.1, bf16[256,128]{1,0:T(8,128)(2,1)} %mg_hbm.1, bf16[3,3,128,128]{3,2,1,0:T(8,128)(2,1)} %cg_hbm.1, s32[15,2,16]{2,1,0:T(2,128)} %bitcast.15, ...), custom_call_target="tpu_custom_call" | custom-call | tf_op jit(solution)/shard_map/glue/pallas_call | solution.py:445
  42.5 2.3 %copy.12 = bf16[1,1,1,4096,128]{4,3,2,1,0:T(8,128)(2,1)} copy(bf16[1,1,1,4096,128]{4,3,2,1,0:T(8,128)(2,1)} %bitcast.13) | data formatting | bytes 2097152

commit v4 on v3

--- a/solution.py
+++ b/solution.py
@@ -24,10 +24,10 @@
 
 
 def kernel(
-    n, x_hbm, ml_hbm, cl_hbm, mg_hbm, cg_hbm, off_hbm, size_hbm, own_hbm, out_ref,
+    n, x_hbm, ml_hbm, cl_hbm, mg_hbm, cg_hbm, off_hbm, size_hbm, own_hbm, out_hbm,
     x_ref, ml_ref, mg_ref, conv_ref, off_ref, size_ref, own_ref,
-    win, wall, bands, smat, pmat, strip, strip_in, canv, canv_in, total_strip, crop, rows, mine, cu, zbuf, wlo, whi,
-    in_s, gr_s, gr_r, zw_s, zw_r, a1_s, a1_r, a2_s, a2_r, r1_s, r1_r, r2_s, r2_r, zc_s, zc_r, m_s, m_r,
+    win, wall, bands, smat, pmat, strip, strip_in, canv, canv_in, total_strip, crop, rows, mine, cu, zbuf, wlo, whi, out_ref,
+    in_s, out_s, gr_s, gr_r, zw_s, zw_r, a1_s, a1_r, a2_s, a2_r, r1_s, r1_r, r2_s, r2_r, zc_s, zc_r, m_s, m_r,
 ):
     tiles = n * n
     br = lax.axis_index("branch")
@@ -317,9 +317,13 @@
         for sft, v in enumerate((left, m, right)):
             zbuf[at, lanes + sft * C : lanes + (sft + 1) * C] = v.reshape(-1, C).astype(BF)
 
+    def out_copy(b):
+        at = pl.ds(b * 512, 512)
+        return pltpu.make_async_copy(out_ref.at[at], out_hbm.at[at], out_s.at[b])
+
     def conv_block(first, hi_first):
-        lo = zbuf[pl.ds(first, 256)]
-        hi = zbuf[pl.ds(hi_first, 256)]
+        lo = zbuf[first : first + 256]
+        hi = zbuf[hi_first : hi_first + 256]
         res = jnp.dot(lo, wlo[...], preferred_element_type=F32)
         res = res + jnp.dot(hi, whi[...], preferred_element_type=F32)
         return res.astype(BF)
@@ -342,34 +346,27 @@
         strips = crop[...].reshape(ROWS * WIN, C)
         cu[...] = jnp.dot(lhs, strips, preferred_element_type=F32).astype(BF).reshape(ROWS, S, C)
 
-        def merge_block(b, carry):
+        for b in range(S // 8):
             ups = []
             for i in range(8):
                 r = (((b * 8 + i) * hh) >> 6) + top
                 ups.append(cu[jnp.clip(r, 0, ROWS - 1)])
-            first = pl.multiple_of(b * 8 * S, 8 * S)
             both = jnp.concatenate(
-                [x_ref[pl.ds(first, 8 * S)], jnp.concatenate(ups, axis=0)], axis=1
+                [x_ref[b * 8 * S : (b + 1) * 8 * S], jnp.concatenate(ups, axis=0)], axis=1
             )
             m = jnp.maximum(jnp.dot(both, weight, preferred_element_type=F32), 0.0)
             for i in range(8):
                 pair = b * 4 + (i + 1) // 2
-                at = pl.ds(pl.multiple_of(pair * S, S), S)
+                at = slice(pair * S, (pair + 1) * S)
                 put(at, 3 * C * ((i + 1) % 2), m[i * S : (i + 1) * S], S)
-            return carry
-
-        lax.fori_loop(0, S // 8, merge_block, 0)
-
-        def conv_step(b, carry):
-            first = pl.multiple_of(b * 256, 256)
-            res = conv_block(first, pl.multiple_of(b * 256 + S, S))
+
+        for b in range(S // 8):
+            res = conv_block(b * 256, b * 256 + S)
             for i in range(4):
                 for o in range(2):
-                    at = pl.ds(pl.multiple_of(b * 512 + (2 * i + o) * S, S), S)
-                    out_ref[at] = res[i * S : (i + 1) * S, o * C : (o + 1) * C]
-            return carry
-
-        lax.fori_loop(0, S // 8, conv_step, 0)
+                    at = b * 512 + (2 * i + o) * S
+                    out_ref[at : at + S] = res[i * S : (i + 1) * S, o * C : (o + 1) * C]
+            out_copy(b).start()
 
     @pl.when(is_root)
     def _():
@@ -404,7 +401,10 @@
                     for o in range(2):
                         at = slice((2 * q + o) * GW, (2 * q + o + 1) * GW)
                         out_ref[at] = res[:, o * C : (o + 1) * C]
-
+                    out_copy(q).start()
+
+    for b in range(8):
+        out_copy(b).wait()
     @pl.when(is_root)
     def _():
         for r in far_first:
@@ -446,7 +446,7 @@
         functools.partial(kernel, n),
         out_shape=jax.ShapeDtypeStruct((CELLS, C), BF),
         in_specs=[hbm] * 8,
-        out_specs=pl.BlockSpec(memory_space=pltpu.VMEM),
+        out_specs=hbm,
         scratch_shapes=[
             vm(CELLS, C),
             vm(2 * C, C),
@@ -472,7 +472,9 @@
             vm(9 * GW, 6 * C),
             vm(6 * C, 2 * C),
             vm(6 * C, 2 * C),
+            vm(CELLS, C),
             dma((7,)),
+            dma((8,)),
             dma((ROWS,)),
             dma((1,)),
             dma((ROWS,)),

time: 44.9 us -> 42.2 us (0.940)
  Pallas kernels: 42.5 us -> 39.8 us
    pallas_call x1, Pallas kernels: 42.5 us -> 39.8 us  [run(): pl.pallas_call(functools.partial(kernel, n), out_shape=jax.ShapeDtypeStru...]
where the time goes in v4:
time: 42.2 us; the launch traced here: 42.1 us
  Pallas kernels  39.8 us (94%)
  local copies, waits for them, and re-layouts  2.26 us (5%)
    pallas_call x1, Pallas kernels, run(): pl.pallas_call(functools.partial(kernel, n), out_shape=jax.ShapeDtypeStru...  39.8 us
    unnamed x1, local copies, waits for them, and re-layouts  2.26 us

profile of v4, /device:TPU:1, one launch (start us, length us, event | category | flops | bytes accessed | tf_op | source)
XLA Modules:
  0.0 42.1 jit_solution(5669867320257516808)
XLA Ops:
  0.0 39.8 %glue.1 = bf16[4096,128]{1,0:T(8,128)(2,1)} custom-call(bf16[4096,128]{1,0:T(8,128)(2,1)} %bitcast.14, bf16[256,128]{1,0:T(8,128)(2,1)} %ml_hbm.1, bf16[3,3,128,128]{3,2,1,0:T(8,128)(2,1)} %cl_hbm.1, bf16[256,128]{1,0:T(8,128)(2,1)} %mg_hbm.1, bf16[3,3,128,128]{3,2,1,0:T(8,128)(2,1)} %cg_hbm.1, s32[15,2,16]{2,1,0:T(2,128)} %bitcast.15, ...), custom_call_target="tpu_custom_call" | custom-call | tf_op jit(solution)/shard_map/glue/pallas_call | solution.py:445
  39.8 2.3 %copy.12 = bf16[1,1,1,4096,128]{4,3,2,1,0:T(8,128)(2,1)} copy(bf16[1,1,1,4096,128]{4,3,2,1,0:T(8,128)(2,1)} %bitcast.13) | data formatting | bytes 2097152

commit v5 on v4

--- a/solution.py
+++ b/solution.py
@@ -24,10 +24,10 @@
 
 
 def kernel(
-    n, x_hbm, ml_hbm, cl_hbm, mg_hbm, cg_hbm, off_hbm, size_hbm, own_hbm, out_hbm,
+    n, x_hbm, ml_hbm, cl_hbm, mg_hbm, cg_hbm, off_hbm, size_hbm, own_hbm, out_ref,
     x_ref, ml_ref, mg_ref, conv_ref, off_ref, size_ref, own_ref,
-    win, wall, bands, smat, pmat, strip, strip_in, canv, canv_in, total_strip, crop, rows, mine, cu, zbuf, wlo, whi, out_ref,
-    in_s, out_s, gr_s, gr_r, zw_s, zw_r, a1_s, a1_r, a2_s, a2_r, r1_s, r1_r, r2_s, r2_r, zc_s, zc_r, m_s, m_r,
+    win, wall, bands, smat, pmat, strip, strip_in, canv, canv_in, total_strip, crop, rows, mine, cu, zbuf, wlo, whi,
+    in_s, gr_s, gr_r, zw_s, zw_r, a1_s, a1_r, a2_s, a2_r, r1_s, r1_r, r2_s, r2_r, zc_s, zc_r, m_s, m_r,
 ):
     tiles = n * n
     br = lax.axis_index("branch")
@@ -317,10 +317,6 @@
         for sft, v in enumerate((left, m, right)):
             zbuf[at, lanes + sft * C : lanes + (sft + 1) * C] = v.reshape(-1, C).astype(BF)
 
-    def out_copy(b):
-        at = pl.ds(b * 512, 512)
-        return pltpu.make_async_copy(out_ref.at[at], out_hbm.at[at], out_s.at[b])
-
     def conv_block(first, hi_first):
         lo = zbuf[first : first + 256]
         hi = zbuf[hi_first : hi_first + 256]
@@ -366,7 +362,6 @@
                 for o in range(2):
                     at = b * 512 + (2 * i + o) * S
                     out_ref[at : at + S] = res[i * S : (i + 1) * S, o * C : (o + 1) * C]
-            out_copy(b).start()
 
     @pl.when(is_root)
     def _():
@@ -401,10 +396,7 @@
                     for o in range(2):
                         at = slice((2 * q + o) * GW, (2 * q + o + 1) * GW)
                         out_ref[at] = res[:, o * C : (o + 1) * C]
-                    out_copy(q).start()
-
-    for b in range(8):
-        out_copy(b).wait()
+
     @pl.when(is_root)
     def _():
         for r in far_first:
@@ -444,9 +436,9 @@
     tiles = n * n
     out = pl.pallas_call(
         functools.partial(kernel, n),
-        out_shape=jax.ShapeDtypeStruct((CELLS, C), BF),
+        out_shape=pltpu.VMEM((CELLS, C), BF),
         in_specs=[hbm] * 8,
-        out_specs=hbm,
+        out_specs=pl.BlockSpec(memory_space=pltpu.VMEM),
         scratch_shapes=[
             vm(CELLS, C),
             vm(2 * C, C),
@@ -472,9 +464,7 @@
             vm(9 * GW, 6 * C),
             vm(6 * C, 2 * C),
             vm(6 * C, 2 * C),
-            vm(CELLS, C),
             dma((7,)),
-            dma((8,)),
             dma((ROWS,)),
             dma((1,)),
             dma((ROWS,)),
@@ -493,14 +483,23 @@
             dma((ROWS + 2,)),
         ],
         compiler_params=pltpu.CompilerParams(
-            collective_id=0, has_side_effects=True, vmem_limit_bytes=58 * 1024 * 1024
+            collective_id=0, has_side_effects=True, vmem_limit_bytes=40 * 1024 * 1024
         ),
         name="glue",
     )(
-        features.reshape(CELLS, C), merge_local, conv_local, merge_global, conv_global,
-        offsets.transpose(0, 2, 3, 1).reshape(SLOTS, 2, tiles),
-        sizes.transpose(0, 2, 3, 1).reshape(SLOTS, 2, tiles),
-        owners.transpose(0, 2, 1),
+        *(
+            pltpu.with_memory_space_constraint(a, pltpu.HBM)
+            for a in (
+                features.reshape(CELLS, C),
+                merge_local,
+                conv_local,
+                merge_global,
+                conv_global,
+                offsets.transpose(0, 2, 3, 1).reshape(SLOTS, 2, tiles),
+                sizes.transpose(0, 2, 3, 1).reshape(SLOTS, 2, tiles),
+                owners.transpose(0, 2, 1),
+            )
+        )
     )
     return out.reshape(features.shape)
 

time: 42.2 us -> 40.2 us (0.953)
  local copies, waits for them, and re-layouts: 2.26 us -> 0.97 us
  Pallas kernels: 39.8 us -> 39.1 us
    unnamed x1, local copies, waits for them, and re-layouts: 2.26 us -> 0.97 us
    pallas_call x1, Pallas kernels: 39.8 us -> 39.1 us  [run(): pl.pallas_call(functools.partial(kernel, n), out_shape=pltpu.VMEM((CELLS,...]
where the time goes in v5:
time: 40.2 us; the launch traced here: 40.1 us
  Pallas kernels  39.1 us (97%)
  local copies, waits for them, and re-layouts  0.97 us (2%)
    pallas_call x1, Pallas kernels, run(): pl.pallas_call(functools.partial(kernel, n), out_shape=pltpu.VMEM((CELLS,...  39.1 us
    unnamed x1, local copies, waits for them, and re-layouts  0.97 us

profile of v5, /device:TPU:1, one launch (start us, length us, event | category | flops | bytes accessed | tf_op | source)
XLA Modules:
  0.0 40.1 jit_solution(857290477883960122)
XLA Ops:
  0.0 39.1 %glue.1 = bf16[4096,128]{1,0:T(8,128)(2,1)S(1)} custom-call(bf16[4096,128]{1,0:T(8,128)(2,1)} %bitcast.14, bf16[256,128]{1,0:T(8,128)(2,1)} %ml_hbm.1, bf16[3,3,128,128]{3,2,1,0:T(8,128)(2,1)} %cl_hbm.1, bf16[256,128]{1,0:T(8,128)(2,1)} %mg_hbm.1, bf16[3,3,128,128]{3,2,1,0:T(8,128)(2,1)} %cg_hbm.1, s32[15,2,16]{2,1,0:T(2,128)} %bitcast.15, ...), custom_call_target="tpu_custom_call" | custom-call | tf_op jit(solution)/shard_map/glue/pallas_call | solution.py:437
  39.1 1.0 %copy.12 = bf16[1,1,1,4096,128]{4,3,2,1,0:T(8,128)(2,1)} copy(bf16[1,1,1,4096,128]{4,3,2,1,0:T(8,128)(2,1)S(1)} %bitcast.13) | data formatting | bytes 2097152

commit v6 on v5

--- a/solution.py
+++ b/solution.py
@@ -30,6 +30,7 @@
     in_s, gr_s, gr_r, zw_s, zw_r, a1_s, a1_r, a2_s, a2_r, r1_s, r1_r, r2_s, r2_r, zc_s, zc_r, m_s, m_r,
 ):
     tiles = n * n
+    peers = sorted(range(1, n), key=lambda d: -min(d, n - d))
     br = lax.axis_index("branch")
     t = lax.axis_index("tile")
     up = br % 2 == 1
@@ -53,8 +54,8 @@
     def greet(b, tile):
         pl.semaphore_signal(barrier, inc=1, device_id=(b, tile), device_id_type=MESH)
 
-    for d in range(1, ROWS):
-        greet((br + d) % ROWS, t)
+    for b in (ROWS - 1, *range(ROWS - 1)):
+        pl.when(br != b)(functools.partial(greet, b, t))
     for d in range(1, n):
         greet(br, ((xx + d) % n) * n + yy)
         greet(br, xx * n + (yy + d) % n)
@@ -133,7 +134,7 @@
         f = xx if r % 2 else yy
         return rc(x_ref.at[r * GW : (r + 1) * GW], bands.at[f], gr_s.at[r], gr_r.at[0], (r, t))
 
-    far_first = (6, 7, 4, 8, 5, 9, 2, 10, 3, 11, 0, 12, 1, 13, 14)
+    far_first = (8, 6, 9, 7, 10, 4, 11, 5, 12, 2, 13, 3, 0, 1, 14)
 
     @pl.when(is_root)
     def _():
@@ -204,21 +205,21 @@
         f = (f0 + d) % n
         rc(bands.at[f], bands.at[f], r1_s.at[d], r1_r.at[f], (br, t)).wait_recv()
 
+    @pl.when(is_local)
+    def _():
+        rc(bands.at[0], bands.at[f0], gr_s.at[0], gr_r.at[0], (br, t)).wait_recv()
+
+    for d in peers:
+        gather_bands(d).start()
+
     for s in range(SLOTS):
 
         @pl.when(br != s)
         def _(s=s):
             rc(win.at[s], wall.at[f0, s], zw_s.at[s], zw_r.at[s], (br, t)).wait_recv()
 
-    for d in range(1, n):
+    for d in peers:
         gather_windows(d).start()
-
-    @pl.when(is_local)
-    def _():
-        rc(bands.at[0], bands.at[f0], gr_s.at[0], gr_r.at[0], (br, t)).wait_recv()
-
-    for d in range(1, n):
-        gather_bands(d).start()
 
     fetches[4].wait()
     fetches[5].wait()
@@ -251,9 +252,22 @@
         rc(strip.at[g], strip_in.at[g], r2_s.at[d], r2_r.at[g], (br, t)).wait_recv()
 
     for d in range(1, n):
+        gather_bands_wait(d)
+    own_strips = None
+    block = SLOTS * WIN
+    for d in [*peers, 0]:
+        g = (g0 + d) % n
+        at = pl.ds(pl.multiple_of(g * block, WIN), block)
+        cut = jnp.dot(smat[at], bands[...].reshape(n * GW, C), preferred_element_type=F32)
+        own_strips = cut.astype(BF).reshape(SLOTS, WIN, C)
+        if d:
+            strip[g] = own_strips
+            scatter_strips(d).start()
+
+    for d in range(1, n):
         gather_windows_wait(d)
     pooled = jnp.zeros((GW, C), F32)
-    for d in [*range(1, n), 0]:
+    for d in [*peers, 0]:
         g = (g0 + d) % n
         pooled = jnp.zeros((GW, C), F32)
         for f in range(n):
@@ -263,18 +277,18 @@
             canv[g] = pooled.astype(BF)
             scatter_canvas(d).start()
 
+    def crop_copy(b):
+        return rc(total_strip.at[b], crop.at[br], zc_s.at[b], zc_r.at[br], (b, t))
+
     for d in range(1, n):
-        gather_bands_wait(d)
-    own_strips = None
-    block = SLOTS * WIN
-    for d in [*range(1, n), 0]:
-        g = (g0 + d) % n
-        at = pl.ds(pl.multiple_of(g * block, WIN), block)
-        cut = jnp.dot(smat[at], bands[...].reshape(n * GW, C), preferred_element_type=F32)
-        own_strips = cut.astype(BF).reshape(SLOTS, WIN, C)
-        if d:
-            strip[g] = own_strips
-            scatter_strips(d).start()
+        scatter_strips_wait(d)
+        own_strips = own_strips + strip_in[(g0 + d) % n]
+    total_strip[0:SLOTS] = own_strips
+    for b in (1, 3, 0, 2, 5, 4, 7, 6, *range(8, SLOTS)):
+
+        @pl.when(br != b)
+        def _(b=b):
+            crop_copy(b).start()
 
     def merged_copy():
         return rc(mine, rows.at[br + 1], m_s.at[0], m_r.at[br + 1], (last, t))
@@ -295,20 +309,6 @@
     pl.when(first_up)(lambda: edge_up().start())
     pl.when(root_down)(lambda: edge_down().start())
 
-    def crop_copy(d):
-        b = (br + d) % ROWS
-        return rc(total_strip.at[b], crop.at[br], zc_s.at[d], zc_r.at[br], (b, t))
-
-    for d in range(1, n):
-        scatter_strips_wait(d)
-        own_strips = own_strips + strip_in[(g0 + d) % n]
-    total_strip[0:SLOTS] = own_strips
-    for d in range(1, ROWS):
-
-        @pl.when((br + d) % ROWS != last)
-        def _(d=d):
-            crop_copy(d).start()
-
     def put(at, lanes, value, width):
         m = value.reshape(-1, width, C)
         col = iota((1, width, 1), 1)
@@ -328,19 +328,23 @@
     def _():
         zbuf[0:S, 0 : 3 * C] = jnp.zeros((S, 3 * C), BF)
         zbuf[S // 2 * S : (S // 2 + 1) * S, 3 * C :] = jnp.zeros((S, 3 * C), BF)
-        s1024 = iota((1024, 1), 0)
-        target = (s1024 // S) * WIN + (((s1024 % S) * ww) >> 6)
-        lhs = jnp.where(iota((1, 256), 1) == target, 1.0, 0.0).astype(BF)
+        s256 = iota((4 * S, 1), 0)
+        target = (s256 // S) * WIN + (((s256 % S) * ww) >> 6)
+        lhs = jnp.where(iota((1, 4 * WIN), 1) == target, 1.0, 0.0).astype(BF)
         weight = ml_ref[...]
         crop[br] = total_strip[slot]
-        for r in range(ROWS):
-
-            @pl.when(br != r)
-            def _(r=r):
-                rc(total_strip.at[0], crop.at[r], zc_s.at[r], zc_r.at[r], (br, t)).wait_recv()
-
-        strips = crop[...].reshape(ROWS * WIN, C)
-        cu[...] = jnp.dot(lhs, strips, preferred_element_type=F32).astype(BF).reshape(ROWS, S, C)
+        order = sorted(range(ROWS), key=lambda d: min(d, ROWS - d))
+        for i in range(0, ROWS, 4):
+            part = [(br + d) % ROWS for d in order[i : i + 4]]
+            for d, r in zip(order[i : i + 4], part):
+                if d:
+                    rc(
+                        total_strip.at[0], crop.at[r], zc_s.at[d], zc_r.at[r], (br, t)
+                    ).wait_recv()
+            strips = jnp.concatenate([crop[r] for r in part], axis=0)
+            wide_rows = jnp.dot(lhs, strips, preferred_element_type=F32).astype(BF)
+            for j, r in enumerate(part):
+                cu[r] = wide_rows[j * S : (j + 1) * S]
 
         for b in range(S // 8):
             ups = []
@@ -413,11 +417,11 @@
         gather_bands(d).wait_send()
         scatter_canvas(d).wait_send()
         scatter_strips(d).wait_send()
-    for d in range(1, ROWS):
-
-        @pl.when((br + d) % ROWS != last)
-        def _(d=d):
-            crop_copy(d).wait_send()
+    for b in range(SLOTS):
+
+        @pl.when(br != b)
+        def _(b=b):
+            crop_copy(b).wait_send()
 
     pl.when(first_up)(lambda: edge_up().wait_send())
     pl.when(root_down)(lambda: edge_down().wait_send())

time: 40.2 us -> 37.8 us (0.940)
  Pallas kernels: 39.1 us -> 36.7 us
    pallas_call x1, Pallas kernels: 39.1 us -> 36.7 us  [run(): pl.pallas_call(functools.partial(kernel, n), out_shape=pltpu.VMEM((CELLS,...]
where the time goes in v6:
time: 37.8 us; the launch traced here: 37.7 us
  Pallas kernels  36.7 us (97%)
  local copies, waits for them, and re-layouts  0.97 us (3%)
    pallas_call x1, Pallas kernels, run(): pl.pallas_call(functools.partial(kernel, n), out_shape=pltpu.VMEM((CELLS,...  36.7 us
    unnamed x1, local copies, waits for them, and re-layouts  0.97 us

profile of v6, /device:TPU:1, one launch (start us, length us, event | category | flops | bytes accessed | tf_op | source)
XLA Modules:
  0.0 37.7 jit_solution(112194080414699712)
XLA Ops:
  0.0 36.7 %glue.1 = bf16[4096,128]{1,0:T(8,128)(2,1)S(1)} custom-call(bf16[4096,128]{1,0:T(8,128)(2,1)} %bitcast.14, bf16[256,128]{1,0:T(8,128)(2,1)} %ml_hbm.1, bf16[3,3,128,128]{3,2,1,0:T(8,128)(2,1)} %cl_hbm.1, bf16[256,128]{1,0:T(8,128)(2,1)} %mg_hbm.1, bf16[3,3,128,128]{3,2,1,0:T(8,128)(2,1)} %cg_hbm.1, s32[15,2,16]{2,1,0:T(2,128)} %bitcast.15, ...), custom_call_target="tpu_custom_call" | custom-call | tf_op jit(solution)/shard_map/glue/pallas_call | solution.py:441
  36.7 1.0 %copy.12 = bf16[1,1,1,4096,128]{4,3,2,1,0:T(8,128)(2,1)} copy(bf16[1,1,1,4096,128]{4,3,2,1,0:T(8,128)(2,1)S(1)} %bitcast.13) | data formatting | bytes 2097152

commit v7 on v6

--- a/solution.py
+++ b/solution.py
@@ -185,8 +185,6 @@
         wall[f, SLOTS] = jnp.zeros((WIN, C), BF)
         return carry
 
-    lax.fori_loop(0, n, place_step, 0)
-    lax.fori_loop(0, n, strip_step, 0)
 
     def gather_windows(d):
         own = wall.at[f0, 0:SLOTS]
@@ -211,6 +209,9 @@
 
     for d in peers:
         gather_bands(d).start()
+
+    lax.fori_loop(0, n, place_step, 0)
+    lax.fori_loop(0, n, strip_step, 0)
 
     for s in range(SLOTS):
 

time: 37.8 us -> 36.6 us (0.968)
  the two profiles are of different devices: /device:TPU:1 before, /device:TPU:32 now
where the time goes in v7:
time: 36.6 us; the launch traced here: 36.4 us
  Pallas kernels  35.5 us (97%)
  local copies, waits for them, and re-layouts  0.97 us (3%)
    pallas_call x1, Pallas kernels, run(): pl.pallas_call(functools.partial(kernel, n), out_shape=pltpu.VMEM((CELLS,...  35.5 us
    unnamed x1, local copies, waits for them, and re-layouts  0.97 us

profile of v7, /device:TPU:32, one launch (start us, length us, event | category | flops | bytes accessed | tf_op | source)
XLA Modules:
  0.0 36.4 jit_solution(13763075231574459266)
XLA Ops:
  0.0 35.5 %glue.1 = bf16[4096,128]{1,0:T(8,128)(2,1)S(1)} custom-call(bf16[4096,128]{1,0:T(8,128)(2,1)} %bitcast.14, bf16[256,128]{1,0:T(8,128)(2,1)} %ml_hbm.1, bf16[3,3,128,128]{3,2,1,0:T(8,128)(2,1)} %cl_hbm.1, bf16[256,128]{1,0:T(8,128)(2,1)} %mg_hbm.1, bf16[3,3,128,128]{3,2,1,0:T(8,128)(2,1)} %cg_hbm.1, s32[15,2,16]{2,1,0:T(2,128)} %bitcast.15, ...), custom_call_target="tpu_custom_call" | custom-call | tf_op jit(solution)/shard_map/glue/pallas_call | solution.py:442
  35.5 1.0 %copy.12 = bf16[1,1,1,4096,128]{4,3,2,1,0:T(8,128)(2,1)} copy(bf16[1,1,1,4096,128]{4,3,2,1,0:T(8,128)(2,1)S(1)} %bitcast.13) | data formatting | bytes 2097152

commit v8 on v7

--- a/solution.py
+++ b/solution.py
@@ -49,6 +49,22 @@
             src_ref=src, dst_ref=dst, send_sem=ss, recv_sem=rs, device_id=dev, device_id_type=MESH
         )
 
+    def fetch(i, src, dst):
+        return pltpu.make_async_copy(src, dst, in_s.at[i])
+
+    fetches = [
+        fetch(0, size_hbm, size_ref),
+        fetch(1, off_hbm, off_ref),
+        fetch(2, own_hbm, own_ref),
+        fetch(3, x_hbm, x_ref),
+        fetch(4, mg_hbm, mg_ref),
+        fetch(5, ml_hbm, ml_ref),
+    ]
+    for f in fetches:
+        f.start()
+    pl.when(is_root)(lambda: fetch(6, cg_hbm, conv_ref).start())
+    pl.when(is_local)(lambda: fetch(6, cl_hbm, conv_ref).start())
+
     barrier = pltpu.get_barrier_semaphore()
 
     def greet(b, tile):
@@ -80,21 +96,6 @@
         greet(0, after)
         greet(last, after)
 
-    def fetch(i, src, dst):
-        return pltpu.make_async_copy(src, dst, in_s.at[i])
-
-    fetches = [
-        fetch(0, size_hbm, size_ref),
-        fetch(1, off_hbm, off_ref),
-        fetch(2, own_hbm, own_ref),
-        fetch(3, x_hbm, x_ref),
-        fetch(4, mg_hbm, mg_ref),
-        fetch(5, ml_hbm, ml_ref),
-    ]
-    for f in fetches:
-        f.start()
-    pl.when(is_root)(lambda: fetch(6, cg_hbm, conv_ref).start())
-    pl.when(is_local)(lambda: fetch(6, cl_hbm, conv_ref).start())
     for f in fetches[:4]:
         f.wait()
 
@@ -149,7 +150,7 @@
 
     @pl.when(is_local)
     def _():
-        for d in range(1, ROWS):
+        for d in sorted(range(1, ROWS), key=lambda d: -min(d, ROWS - d)):
             window_copy(d).start()
         wall[f0, slot] = win[br]
 
@@ -203,6 +204,8 @@
         f = (f0 + d) % n
         rc(bands.at[f], bands.at[f], r1_s.at[d], r1_r.at[f], (br, t)).wait_recv()
 
+    lax.fori_loop(0, n, strip_step, 0)
+
     @pl.when(is_local)
     def _():
         rc(bands.at[0], bands.at[f0], gr_s.at[0], gr_r.at[0], (br, t)).wait_recv()
@@ -211,7 +214,6 @@
         gather_bands(d).start()
 
     lax.fori_loop(0, n, place_step, 0)
-    lax.fori_loop(0, n, strip_step, 0)
 
     for s in range(SLOTS):
 
@@ -309,6 +311,22 @@
     pl.when(is_local)(lambda: merged_copy().start())
     pl.when(first_up)(lambda: edge_up().start())
     pl.when(root_down)(lambda: edge_down().start())
+
+    @pl.when(is_root)
+    def _():
+        for r in far_first:
+            row_copy(r).wait_send()
+
+    @pl.when(is_local)
+    def _():
+        for d in range(1, ROWS):
+            window_copy(d).wait_send()
+
+    for d in range(1, n):
+        gather_windows(d).wait_send()
+        gather_bands(d).wait_send()
+        scatter_canvas(d).wait_send()
+        scatter_strips(d).wait_send()
 
     def put(at, lanes, value, width):
         m = value.reshape(-1, width, C)
@@ -402,22 +420,7 @@
                         at = slice((2 * q + o) * GW, (2 * q + o + 1) * GW)
                         out_ref[at] = res[:, o * C : (o + 1) * C]
 
-    @pl.when(is_root)
-    def _():
-        for r in far_first:
-            row_copy(r).wait_send()
-
-    @pl.when(is_local)
-    def _():
-        for d in range(1, ROWS):
-            window_copy(d).wait_send()
-        merged_copy().wait_send()
-
-    for d in range(1, n):
-        gather_windows(d).wait_send()
-        gather_bands(d).wait_send()
-        scatter_canvas(d).wait_send()
-        scatter_strips(d).wait_send()
+    pl.when(is_local)(lambda: merged_copy().wait_send())
     for b in range(SLOTS):
 
         @pl.when(br != b)

time: 36.6 us -> 36.5 us (level)
  no operation moved by 1% of the time
where the time goes in v8:
time: 36.5 us; the launch traced here: 36.3 us
  Pallas kernels  35.3 us (97%)
  local copies, waits for them, and re-layouts  0.97 us (3%)
    pallas_call x1, Pallas kernels, run(): pl.pallas_call(functools.partial(kernel, n), out_shape=pltpu.VMEM((CELLS,...  35.3 us
    unnamed x1, local copies, waits for them, and re-layouts  0.97 us

profile of v8, /device:TPU:32, one launch (start us, length us, event | category | flops | bytes accessed | tf_op | source)
XLA Modules:
  0.0 36.3 jit_solution(11210046643943238331)
XLA Ops:
  0.0 35.3 %glue.1 = bf16[4096,128]{1,0:T(8,128)(2,1)S(1)} custom-call(bf16[4096,128]{1,0:T(8,128)(2,1)} %bitcast.14, bf16[256,128]{1,0:T(8,128)(2,1)} %ml_hbm.1, bf16[3,3,128,128]{3,2,1,0:T(8,128)(2,1)} %cl_hbm.1, bf16[256,128]{1,0:T(8,128)(2,1)} %mg_hbm.1, bf16[3,3,128,128]{3,2,1,0:T(8,128)(2,1)} %cg_hbm.1, s32[15,2,16]{2,1,0:T(2,128)} %bitcast.15, ...), custom_call_target="tpu_custom_call" | custom-call | tf_op jit(solution)/shard_map/glue/pallas_call | solution.py:445
  35.3 1.0 %copy.12 = bf16[1,1,1,4096,128]{4,3,2,1,0:T(8,128)(2,1)} copy(bf16[1,1,1,4096,128]{4,3,2,1,0:T(8,128)(2,1)S(1)} %bitcast.13) | data formatting | bytes 2097152

commit v9 on v8

--- a/solution.py
+++ b/solution.py
@@ -213,7 +213,6 @@
     for d in peers:
         gather_bands(d).start()
 
-    lax.fori_loop(0, n, place_step, 0)
 
     for s in range(SLOTS):
 
@@ -267,6 +266,7 @@
             strip[g] = own_strips
             scatter_strips(d).start()
 
+    lax.fori_loop(0, n, place_step, 0)
     for d in range(1, n):
         gather_windows_wait(d)
     pooled = jnp.zeros((GW, C), F32)
@@ -403,7 +403,7 @@
 
         here = set()
         done = set()
-        for i in (16, 15, 1, 2, 13, 14, 3, 4, 11, 12, 5, 6, 9, 10, 0, 17, 7, 8):
+        for i in (16, 15, 7, 8, 9, 10, 5, 6, 11, 12, 3, 4, 13, 14, 0, 17, 1, 2):
             if i == 0:
                 pl.when(has_before)(functools.partial(wait, 0))
             elif i == ROWS + 1:

time: 36.5 us -> 35.8 us (0.981)
  the two profiles are of different devices: /device:TPU:32 before, /device:TPU:1 now
where the time goes in v9:
time: 35.8 us; the launch traced here: 35.7 us
  Pallas kernels  34.7 us (97%)
  local copies, waits for them, and re-layouts  0.97 us (3%)
    pallas_call x1, Pallas kernels, run(): pl.pallas_call(functools.partial(kernel, n), out_shape=pltpu.VMEM((CELLS,...  34.7 us
    unnamed x1, local copies, waits for them, and re-layouts  0.97 us

profile of v9, /device:TPU:1, one launch (start us, length us, event | category | flops | bytes accessed | tf_op | source)
XLA Modules:
  0.0 35.7 jit_solution(12855722914299074882)
XLA Ops:
  0.0 34.7 %glue.1 = bf16[4096,128]{1,0:T(8,128)(2,1)S(1)} custom-call(bf16[4096,128]{1,0:T(8,128)(2,1)} %bitcast.14, bf16[256,128]{1,0:T(8,128)(2,1)} %ml_hbm.1, bf16[3,3,128,128]{3,2,1,0:T(8,128)(2,1)} %cl_hbm.1, bf16[256,128]{1,0:T(8,128)(2,1)} %mg_hbm.1, bf16[3,3,128,128]{3,2,1,0:T(8,128)(2,1)} %cg_hbm.1, s32[15,2,16]{2,1,0:T(2,128)} %bitcast.15, ...), custom_call_target="tpu_custom_call" | custom-call | tf_op jit(solution)/shard_map/glue/pallas_call | solution.py:445
  34.7 1.0 %copy.12 = bf16[1,1,1,4096,128]{4,3,2,1,0:T(8,128)(2,1)} copy(bf16[1,1,1,4096,128]{4,3,2,1,0:T(8,128)(2,1)S(1)} %bitcast.13) | data formatting | bytes 2097152

commit v10 on v9

--- a/solution.py
+++ b/solution.py
@@ -204,8 +204,6 @@
         f = (f0 + d) % n
         rc(bands.at[f], bands.at[f], r1_s.at[d], r1_r.at[f], (br, t)).wait_recv()
 
-    lax.fori_loop(0, n, strip_step, 0)
-
     @pl.when(is_local)
     def _():
         rc(bands.at[0], bands.at[f0], gr_s.at[0], gr_r.at[0], (br, t)).wait_recv()
@@ -213,6 +211,7 @@
     for d in peers:
         gather_bands(d).start()
 
+    lax.fori_loop(0, n, strip_step, 0)
 
     for s in range(SLOTS):
 

time: 35.8 us -> 35.8 us (level)
  no operation moved by 1% of the time
where the time goes in v10:
time: 35.8 us; the launch traced here: 35.7 us
  Pallas kernels  34.7 us (97%)
  local copies, waits for them, and re-layouts  0.97 us (3%)
    pallas_call x1, Pallas kernels, run(): pl.pallas_call(functools.partial(kernel, n), out_shape=pltpu.VMEM((CELLS,...  34.7 us
    unnamed x1, local copies, waits for them, and re-layouts  0.97 us

profile of v10, /device:TPU:1, one launch (start us, length us, event | category | flops | bytes accessed | tf_op | source)
XLA Modules:
  0.0 35.7 jit_solution(15286827595329480864)
XLA Ops:
  0.0 34.7 %glue.1 = bf16[4096,128]{1,0:T(8,128)(2,1)S(1)} custom-call(bf16[4096,128]{1,0:T(8,128)(2,1)} %bitcast.14, bf16[256,128]{1,0:T(8,128)(2,1)} %ml_hbm.1, bf16[3,3,128,128]{3,2,1,0:T(8,128)(2,1)} %cl_hbm.1, bf16[256,128]{1,0:T(8,128)(2,1)} %mg_hbm.1, bf16[3,3,128,128]{3,2,1,0:T(8,128)(2,1)} %cg_hbm.1, s32[15,2,16]{2,1,0:T(2,128)} %bitcast.15, ...), custom_call_target="tpu_custom_call" | custom-call | tf_op jit(solution)/shard_map/glue/pallas_call | solution.py:444
  34.7 1.0 %copy.12 = bf16[1,1,1,4096,128]{4,3,2,1,0:T(8,128)(2,1)} copy(bf16[1,1,1,4096,128]{4,3,2,1,0:T(8,128)(2,1)S(1)} %bitcast.13) | data formatting | bytes 2097152
